TPU v7x, 32 devices: a whole 2x2x4 slice. The times are simulated.
32 devices in a mesh: wide: 8 (over y, x, core), narrow: 4 (over z).
Axes of the slice: x: 2, y: 2, z: 4, core: 2. Of those that a mesh axis runs over, the one named last changes fastest.
Arguments:
- coarse_basis: bfloat16 [16, 96, 3, 16, 8, 128], P('wide', None, None, 'narrow')
- material_ids: int32 [16, 16, 8, 128], P('wide', 'narrow'), may hold values from 0 to 15
- lame_table: bfloat16 [2, 16], replicated, may hold values from 0.5 to 4
- coarse_ids: int32 [16, 96], P('wide'), may hold values from 0 to 127, as said below
- coarse_slab: bfloat16 [98304, 512], P('wide', 'narrow'), may hold values from -0.5 to 2.5, as said below
- panel_owner: int32 [1], replicated, may hold values from 0 to 2
Outputs:
- factored: bfloat16 [98304, 512], P('wide', 'narrow')
- galerkin: float32 [16, 96, 96], P('wide')
Inputs may be any that keep to these rules, and one draw needn't show every extreme that they name: `coarse_ids`: the 96 numbers of a row are distinct. `coarse_slab`: for every column block t, the 128 x 128 block whose rows begin at t * 2 * 12288 is symmetric positive definite.
All inputs are finite; a program needn't handle non-finite values.
Results may differ from a plain program's by a relative error of at most 0.001.
The roundings to bfloat16 on the way count: a program that leaves them out, or rounds other values in their place, can miss the bound.
Values may be sent and summed in bfloat16 or wider, within the bound.
No kernel may reach another device: no remote copies, remote signals or barrier semaphores. Data moves between devices by JAX's collectives and lax.ppermute only.
A program may use at most 192 MiB of HBM per device.

v0:
```python
import functools

import jax
import jax.numpy as jnp
from jax import lax
from jax.experimental import pallas as pl
from jax.experimental.pallas import tpu as pltpu
from jax.sharding import PartitionSpec as P

F32, BF16 = jnp.float32, jnp.bfloat16
NT = (((1,), (1,)), ((), ()))
TN = (((0,), (0,)), ((), ()))
VMEM = pl.BlockSpec(memory_space=pltpu.VMEM)
ANY = pl.BlockSpec(memory_space=pl.ANY)
SMEM = pl.BlockSpec(memory_space=pltpu.SMEM)
PLANS = {
    1: (
        (12, 10, 2),
        (),
        ((0, 0), "assemble", "spread", "others", "spread", "more", "spread", "factor", ("panel", 1, 2), ("panel", 0, 1), ("panel", 2, 3)),
    ),
    2: (
        (12, 6, 4, 2),
        (),
        (
            (0, 0), "assemble", "spread", "others", "spread", "more", "spread", (1, 0), "factor",
            (2, 0), ("panel", 1, 2), (3, 0), ("panel", 2, 3), ("panel", 0, 1), ("panel", 3, 4),
        ),
    ),
    3: (
        (12, 4, 4, 2, 2),
        (1, 2, 3),
        (
            (0, 0), "assemble", "spread", "others", "spread", "more", "spread", "factor",
            (1, 0), (1, 1), (0, 1), (2, 0), (2, 1), (3, 0), ("panel", 1, 2), (3, 1), (4, 0), ("panel", 2, 3), (4, 1),
            ("panel", 0, 1), ("panel", 3, 5),
        ),
    ),
}
BLOCK = 16
LIGHT = pl.CostEstimate(flops=1, bytes_accessed=1, transcendentals=0)


def exact_dot(left, right, dims=(((1,), (0,)), ((), ()))):
    return lax.dot_general(
        left, right, dims, precision=lax.Precision.HIGHEST, preferred_element_type=F32
    )


def dot(left, right, dims=(((1,), (0,)), ((), ()))):
    return lax.dot_general(left, right, dims, preferred_element_type=F32)


def split_two(value):
    high = value.astype(BF16)
    return high, (value - high.astype(F32)).astype(BF16)


def lame_of(ids, table_ref):
    shear = jnp.zeros(ids.shape, F32)
    dilate = jnp.zeros(ids.shape, F32)
    for material in range(table_ref.shape[1]):
        chosen = ids == material
        shear = jnp.where(chosen, table_ref[0, material], shear)
        dilate = jnp.where(chosen, table_ref[1, material], dilate)
    return shear, dilate


def halo_kernel(table_ref, ids_ref, token_ref, basis_ref, slab_ref, out_ref, last_ref, *rest, spans):
    piece_refs, sems = rest[:-1], rest[-1]
    subs, funcs, comps, layers = basis_ref.shape[0:4]
    copies = []
    for number, ((low, high), piece_ref) in enumerate(zip(spans, piece_refs)):
        copies.append(pltpu.make_async_copy(slab_ref.at[pl.ds(low, high - low)], piece_ref, sems.at[number]))
        copies[-1].start()
    for sub in range(subs):
        for comp in range(comps):
            out_ref[sub, comp * funcs : (comp + 1) * funcs] = basis_ref[sub, :, comp, 0]
            last_ref[sub, comp * funcs : (comp + 1) * funcs] = basis_ref[sub, :, comp, layers - 1]
        shear, dilate = lame_of(ids_ref[sub, 0], table_ref)
        out_ref[sub, comps * funcs] = shear.astype(BF16)
        out_ref[sub, comps * funcs + 1] = dilate.astype(BF16)
    for copy in copies:
        copy.wait()


def halo_message(table, ids, token, basis, slab, spans):
    subs, funcs, comps, layers, ny, nz = basis.shape
    return pl.pallas_call(
        functools.partial(halo_kernel, spans=spans),
        in_specs=[SMEM, VMEM, ANY, VMEM, ANY],
        out_specs=[VMEM] * (2 + len(spans)),
        out_shape=[
            jax.ShapeDtypeStruct((subs, comps * funcs + 2, ny, nz), BF16),
            jax.ShapeDtypeStruct((subs, comps * funcs, ny, nz), BF16),
        ]
        + [jax.ShapeDtypeStruct((high - low, slab.shape[1]), BF16) for low, high in spans],
        scratch_shapes=[pltpu.SemaphoreType.DMA((max(1, len(spans)),))],
        compiler_params=pltpu.CompilerParams(vmem_limit_bytes=16 * 2**20),
        cost_estimate=LIGHT,
        name="halo_message",
    )(table, ids, token, basis, slab)


def interior_kernel(edge_ref, table_ref, ids_ref, basis_ref, token_ref, out_ref, fields, turned, coef, left, right, acc):
    sub, comp = pl.program_id(0), pl.program_id(1)
    layers, ny, nz = basis_ref.shape[3:]
    funcs = basis_ref.shape[1]
    row = lax.broadcasted_iota(jnp.int32, (ny, nz), 0)
    lane = lax.broadcasted_iota(jnp.int32, (ny, nz), 1)
    table = [lame_of(ids_ref[sub, x], table_ref) for x in range(layers)]

    def weight(one, two, direction):
        shear = 0.5 * (one[0] + two[0])
        dilate = 0.5 * (one[1] + two[1])
        return shear + jnp.where(comp == direction, shear + dilate, 0.0)

    def ahead(field, axis):
        size = field.shape[axis]
        index = row if axis == 0 else lane
        return jnp.where(index == size - 1, 0.0, pltpu.roll(field, size - 1, axis=axis))

    def behind(field, axis):
        index = row if axis == 0 else lane
        return jnp.where(index == 0, 0.0, pltpu.roll(field, 1, axis=axis))

    nothing = (jnp.zeros((ny, nz), F32),) * 2
    previous = weight(table[0], nothing, 0) * edge_ref[0].astype(F32)
    for x in range(layers):
        diagonal = previous
        forward = []
        if x + 1 < layers:
            face = weight(table[x], table[x + 1], 0)
            diagonal = diagonal + face
            previous = face
            forward.append(face)
        else:
            forward.append(jnp.zeros((ny, nz), F32))
        for axis in (0, 1):
            index, size = (row, ny) if axis == 0 else (lane, nz)
            other = tuple(ahead(value, axis) for value in table[x])
            face = weight(table[x], other, axis + 1)
            before = tuple(behind(value, axis) for value in table[x])
            diagonal = diagonal + face + weight(table[x], before, axis + 1)
            forward.append(jnp.where(index == size - 1, 0.0, face))
        coef[x, 0] = 0.5 * diagonal
        for kind in range(3):
            coef[x, kind + 1] = forward[kind]
        fields[x] = basis_ref[sub, :, comp, x].astype(F32).reshape(funcs * ny, nz)

    total = None
    for x in reversed(range(layers)):
        values = [fields[x, pl.ds(y, funcs, stride=ny), :] for y in range(ny)]
        for y in range(ny):
            value = values[y]
            turned[x % 2, y] = value
            image = coef[x, 0, y : y + 1, :] * value
            image = image - coef[x, 3, y : y + 1, :] * pltpu.roll(value, nz - 1, axis=1)
            if y + 1 < ny:
                image = image - coef[x, 2, y : y + 1, :] * values[y + 1]
            if x + 1 < layers:
                image = image - coef[x, 1, y : y + 1, :] * turned[(x + 1) % 2, y]
            high, low = split_two(image)
            left[:, y * nz : (y + 1) * nz] = value.astype(BF16)
            right[0:funcs, y * nz : (y + 1) * nz] = high
            right[funcs : 2 * funcs, y * nz : (y + 1) * nz] = low
        product = dot(right[...], left[...], NT)
        total = product if total is None else total + product

    @pl.when(comp == 0)
    def _():
        acc[...] = total

    @pl.when(comp > 0)
    def _():
        acc[...] += total

    @pl.when(comp == pl.num_programs(1) - 1)
    def _():
        out_ref[0] = acc[0:funcs] + acc[funcs : 2 * funcs]


def interior(edge, table, ids, basis, token):
    subs, funcs, comps, layers, ny, nz = basis.shape
    return pl.pallas_call(
        interior_kernel,
        grid=(subs, comps),
        in_specs=[SMEM, SMEM, VMEM, VMEM, ANY],
        out_specs=pl.BlockSpec((1, funcs, funcs), lambda s, c: (s, 0, 0)),
        out_shape=jax.ShapeDtypeStruct((subs, funcs, funcs), F32),
        scratch_shapes=[
            pltpu.VMEM((layers, funcs * ny, nz), F32),
            pltpu.VMEM((2, ny, funcs, nz), F32),
            pltpu.VMEM((layers, 4, ny, nz), F32),
            pltpu.VMEM((funcs, ny * nz), BF16),
            pltpu.VMEM((2 * funcs, ny * nz), BF16),
            pltpu.VMEM((2 * funcs, funcs), F32),
        ],
        compiler_params=pltpu.CompilerParams(vmem_limit_bytes=16 * 2**20),
        cost_estimate=LIGHT,
        name="interior",
    )(edge, table, ids, basis, token)


def face_kernel(flags_ref, table_ref, ids_ref, last_ref, halo_ref, token_ref, inner_ref, out_ref, *scratch):
    @pl.when(flags_ref[0] == 1)
    def _():
        last, halo, sems = scratch[-3:]
        copies = [
            pltpu.make_async_copy(last_ref, last, sems.at[0]),
            pltpu.make_async_copy(halo_ref, halo, sems.at[1]),
        ]
        for copy in copies:
            copy.start()
        for copy in copies:
            copy.wait()
        face_sums(table_ref, ids_ref, last, halo, inner_ref, out_ref, *scratch[:-3])


def face_sums(table_ref, ids_ref, last_ref, halo_ref, inner_ref, out_ref, mine, theirs, left, right, weights, acc):
    subs, layers, ny, nz = ids_ref.shape
    funcs = inner_ref.shape[1]
    comps = last_ref.shape[1] // funcs

    @pl.loop(0, subs)
    def _(sub):
        shear, dilate = lame_of(ids_ref[sub, layers - 1], table_ref)
        weights[0] = 0.5 * (shear + halo_ref[sub, comps * funcs].astype(F32))
        weights[1] = 0.5 * (dilate + halo_ref[sub, comps * funcs + 1].astype(F32))

        @pl.loop(0, comps)
        def _(comp):
            weight = weights[0] + jnp.where(comp == 0, weights[0] + weights[1], 0.0)
            rows = pl.ds(comp * funcs, funcs)
            mine[...] = last_ref[sub, rows].astype(F32).reshape(funcs * ny, nz)
            theirs[...] = halo_ref[sub, rows].astype(F32).reshape(funcs * ny, nz)
            for y in range(ny):
                here = mine[pl.ds(y, funcs, stride=ny), :]
                there = theirs[pl.ds(y, funcs, stride=ny), :]
                high, low = split_two(weight[y : y + 1, :] * (here - there))
                left[0:funcs, y * nz : (y + 1) * nz] = here.astype(BF16)
                left[funcs : 2 * funcs, y * nz : (y + 1) * nz] = there.astype(BF16)
                right[0:funcs, y * nz : (y + 1) * nz] = high
                right[funcs : 2 * funcs, y * nz : (y + 1) * nz] = low
            product = dot(right[...], left[...], NT)

            @pl.when(comp == 0)
            def _():
                acc[...] = product

            @pl.when(comp > 0)
            def _():
                acc[...] += product

        total = acc[:, 0:funcs] - acc[:, funcs : 2 * funcs]
        half = inner_ref[sub] + 0.5 * (total[0:funcs] + total[funcs : 2 * funcs])
        out_ref[sub] = half + half.T


def face(flags, table, ids, last, halo, token, inner):
    subs, layers, ny, nz = ids.shape
    funcs = inner.shape[1]
    return pl.pallas_call(
        face_kernel,
        in_specs=[SMEM, SMEM, VMEM, ANY, ANY, ANY, VMEM],
        out_specs=VMEM,
        out_shape=jax.ShapeDtypeStruct((subs, funcs, funcs), F32),
        scratch_shapes=[
            pltpu.VMEM((funcs * ny, nz), F32),
            pltpu.VMEM((funcs * ny, nz), F32),
            pltpu.VMEM((2 * funcs, ny * nz), BF16),
            pltpu.VMEM((2 * funcs, ny * nz), BF16),
            pltpu.VMEM((2, ny, nz), F32),
            pltpu.VMEM((2 * funcs, 2 * funcs), F32),
            pltpu.VMEM(last.shape, BF16),
            pltpu.VMEM(halo.shape, BF16),
            pltpu.SemaphoreType.DMA((2,)),
        ],
        compiler_params=pltpu.CompilerParams(vmem_limit_bytes=16 * 2**20),
        cost_estimate=LIGHT,
        name="face",
    )(flags, table, ids, last, halo, token, inner)


def spread(gal_ref, column_ids_ref, row_ids_ref, size):
    subs, funcs = column_ids_ref.shape[0:2]
    added = jnp.zeros((size, size), F32)
    lane = lax.broadcasted_iota(jnp.int32, (funcs, size), 1)
    row = lax.broadcasted_iota(jnp.int32, (size, funcs), 0)
    for sub in range(subs):
        slots = (column_ids_ref[sub] == lane).astype(F32)
        slots_t = (row_ids_ref[sub] == row).astype(F32)
        added = added + exact_dot(slots_t, exact_dot(gal_ref[sub], slots))
    return added


def assemble_kernel(flags_ref, token_ref, column_ids_ref, row_ids_ref, slab_ref, head_ref, *rest):
    gal_refs, (message_ref, sum_ref) = rest[:-2], rest[-2:]
    size = message_ref.shape[0]
    mode, own = flags_ref[0], flags_ref[1]
    message_ref[...] = jnp.zeros_like(message_ref)

    @pl.when((mode == 1) & (own == 1))
    def _():
        total = gal_refs[0][...]
        for gal_ref in gal_refs[1:]:
            total = total + gal_ref[...]
        sum_ref[...] = total
        added = spread(sum_ref, column_ids_ref, row_ids_ref, size)
        message_ref[...] = added + slab_ref[...].astype(F32)

    @pl.when((mode == 2) & (own == 1))
    def _():
        message_ref[...] = head_ref[...].astype(F32)


def assemble(flags, token, ids, slab, head, parts):
    size = slab.shape[1]
    block = pl.BlockSpec((size, size), lambda i: (0, 0))
    return pl.pallas_call(
        assemble_kernel,
        grid=(1,),
        in_specs=[SMEM, ANY, VMEM, VMEM, block, block] + [VMEM] * len(parts),
        out_specs=VMEM,
        out_shape=jax.ShapeDtypeStruct((size, size), F32),
        scratch_shapes=[pltpu.VMEM(parts[0].shape, F32)],
        cost_estimate=LIGHT,
        name="assemble",
    )(flags, token, ids[:, :, None], ids[:, None, :], slab, head, *parts)


def factor_kernel(flags_ref, token_ref, *refs, parts, groups):
    message_refs, gal_refs = refs[:parts], refs[parts:-4]
    summary_ref, block_ref, sum_ref, work = refs[-4:]
    subs, funcs = gal_refs[0].shape[0:2]
    size = summary_ref.shape[1]
    diagonal = message_refs[0][...]
    for message_ref in message_refs[1:]:
        diagonal = diagonal + message_ref[...]
    block_ref[...] = diagonal

    @pl.when(flags_ref[0] == 1)
    def _():
        row = lax.broadcasted_iota(jnp.int32, (size, size), 0)
        lane = lax.broadcasted_iota(jnp.int32, (size, size), 1)
        work[:, 0:size] = 0.5 * (diagonal + diagonal.T)
        work[:, size : 2 * size] = (row == lane).astype(F32)
        index = lax.broadcasted_iota(jnp.int32, (BLOCK, size), 0)
        for start in range(0, size, BLOCK):
            panel = work[start : start + BLOCK, 0:size]
            extra = work[start : start + BLOCK, size : 2 * size]
            columns = [
                jnp.broadcast_to(panel[:, start + step : start + step + 1], (BLOCK, size))
                for step in range(BLOCK)
            ]
            for step in range(BLOCK):
                scale = lax.rsqrt(columns[step][step : step + 1, :])
                column = jnp.where(index > step, columns[step] * scale, 0.0)
                for later in range(step + 1, BLOCK):
                    columns[later] = columns[later] - column * column[later : later + 1, :]
                pivot = panel[step : step + 1, :] * scale
                panel = jnp.where(index == step, pivot, panel - column * pivot)
                pivot = extra[step : step + 1, :] * scale
                extra = jnp.where(index == step, pivot, extra - column * pivot)
            work[start : start + BLOCK, 0:size] = panel
            work[start : start + BLOCK, size : 2 * size] = extra
            rest = start + BLOCK
            if rest < size:
                both = jnp.concatenate([panel, extra], axis=1)
                work[rest:size, :] -= exact_dot(panel[:, rest:size], both, TN)
        upper = jnp.where(row <= lane, work[:, 0:size], 0.0)
        inverse = jnp.where(row >= lane, work[:, size : 2 * size], 0.0).T
        high = inverse.astype(BF16)
        summary_ref[0:size] = high
        summary_ref[size : 2 * size] = (inverse - high.astype(F32)).astype(BF16)
        summary_ref[2 * size : 3 * size] = upper.T.astype(BF16)
        each = len(gal_refs) // groups
        for group in range(groups):

            @pl.when(flags_ref[1] == group)
            def _(chosen=gal_refs[group * each : (group + 1) * each]):
                total = chosen[0][...]
                for gal_ref in chosen[1:]:
                    total = total + gal_ref[...]
                sum_ref[...] = total


def factorize(flags, token, messages, groups):
    size = messages[0].shape[1]
    subs, funcs = groups[0][0].shape[0:2]
    parts = [part for group in groups for part in group]
    return pl.pallas_call(
        functools.partial(factor_kernel, parts=len(messages), groups=len(groups)),
        in_specs=[SMEM, ANY] + [VMEM] * (len(messages) + len(parts)),
        out_specs=[VMEM] * 3,
        out_shape=[
            jax.ShapeDtypeStruct((3 * size, size), BF16),
            jax.ShapeDtypeStruct((size, size), F32),
            jax.ShapeDtypeStruct(groups[0][0].shape, F32),
        ],
        scratch_shapes=[pltpu.VMEM((size, 2 * size), F32)],
        cost_estimate=LIGHT,
        name="factorize",
    )(flags, token, *messages, *parts)


def prepare_kernel(flags_ref, token_ref, head_ref, *rest, sources):
    summary_refs = rest[:sources]
    weights_ref, rows_ref, lower_ref, summary, sem = rest[sources:]
    size = head_ref.shape[0]
    choice, mode = flags_ref[0], flags_ref[1]
    for number, summary_ref in enumerate(summary_refs):

        @pl.when(choice == number)
        def _(summary_ref=summary_ref):
            copy = pltpu.make_async_copy(summary_ref, summary, sem)
            copy.start()
            copy.wait()

    def doubled(block):
        nothing = jnp.zeros((size, size), BF16)
        top = jnp.concatenate([block, nothing], axis=1)
        return jnp.concatenate([top, jnp.concatenate([nothing, block], axis=1)], axis=0)

    @pl.when(mode > 0)
    def _():
        weights_ref[0 : 2 * size] = doubled(summary[0:size])
        weights_ref[2 * size : 4 * size] = doubled(summary[size : 2 * size])
        lower_ref[...] = summary[2 * size : 3 * size]

    @pl.when(mode == 2)
    def _():
        inverse = summary[0:size].astype(F32) + summary[size : 2 * size].astype(F32)
        solved = exact_dot(head_ref[...], inverse)
        rows_ref[...] = doubled(solved.T.astype(BF16))


def prepare(flags, token, head, summaries):
    size = head.shape[0]
    return pl.pallas_call(
        functools.partial(prepare_kernel, sources=len(summaries)),
        in_specs=[SMEM, ANY, VMEM] + [ANY] * len(summaries),
        out_specs=[VMEM] * 3,
        out_shape=[
            jax.ShapeDtypeStruct((4 * size, 2 * size), BF16),
            jax.ShapeDtypeStruct((2 * size, 2 * size), BF16),
            jax.ShapeDtypeStruct((size, size), BF16),
        ],
        scratch_shapes=[pltpu.VMEM(summaries[0].shape, BF16), pltpu.SemaphoreType.DMA],
        compiler_params=pltpu.CompilerParams(vmem_limit_bytes=16 * 2**20),
        cost_estimate=LIGHT,
        name="prepare",
    )(flags, token, head, *summaries)


def added_kernel(flags_ref, token_ref, column_ids_ref, row_ids_ref, *rest, sources):
    sum_refs, (added_ref, gal_ref) = rest[:sources], rest[sources:]
    for number, sum_ref in enumerate(sum_refs):

        @pl.when(flags_ref[0] == number)
        def _(sum_ref=sum_ref):
            gal_ref[...] = sum_ref[...]

    @pl.when((flags_ref[1] == 2) & (flags_ref[2] == 1))
    def _():
        added_ref[...] = spread(gal_ref, column_ids_ref, row_ids_ref, added_ref.shape[0])


def added_of(flags, token, ids, sums, size):
    return pl.pallas_call(
        functools.partial(added_kernel, sources=len(sums)),
        in_specs=[SMEM, ANY] + [VMEM] * (2 + len(sums)),
        out_specs=[VMEM] * 2,
        out_shape=[jax.ShapeDtypeStruct((size, size), F32), jax.ShapeDtypeStruct(sums[0].shape, F32)],
        cost_estimate=LIGHT,
        name="added",
    )(flags, token, ids[:, :, None], ids[:, None, :], *sums)


def panel_kernel(
    flags_ref, token_ref, lower_ref, weights_ref, rows_ref, added_ref, slab_ref, *rest, pieces, spans, first
):
    hops = len(pieces) // len(spans)
    others = rest[: len(pieces)]
    out_ref, done_ref, column, factor, sems = rest[-5:]
    done_ref[0] = flags_ref[0]
    tile, size = out_ref.shape
    half = tile // 2
    mode, head, own, which = flags_ref[0], flags_ref[1], flags_ref[2], flags_ref[3]
    step, steps = pl.program_id(0), pl.num_programs(0)
    top = first & (step == 0)

    def copy_of(at, act):
        for number, (begin, end) in enumerate(spans):
            for hop in range(hops):

                @pl.when((mode == 2) & (which == hop) & (at >= begin) & (at < end))
                def _(other_ref=others[number * hops + hop], begin=begin):
                    source = other_ref.at[pl.ds(pl.multiple_of((at - begin) * tile, tile), tile)]
                    act(pltpu.make_async_copy(source, column.at[at % 2], sems.at[at % 2]))

    @pl.when(step == 0)
    def _():
        copy_of(step, lambda copy: copy.start())

    @pl.when(step + 1 < steps)
    def _():
        copy_of(step + 1, lambda copy: copy.start())

    @pl.when(mode == 0)
    def _():
        out_ref[...] = slab_ref[...]

    @pl.when(mode == 1)
    def _():
        column[step % 2] = slab_ref[...]

    @pl.when(mode == 2)
    def _():
        copy_of(step, lambda copy: copy.wait())

    @pl.when(mode > 0)
    def _():
        value = column[step % 2]
        pair = jnp.concatenate([value[0:half], value[half:tile]], axis=1)
        factor[...] = dot(jnp.concatenate([pair, pair], axis=1), weights_ref[...]).astype(BF16)

        @pl.when(top & (head == 1))
        def _():
            factor[0:size, 0:size] = lower_ref[...]

        @pl.when(top & (head == 2))
        def _():
            factor[0:size, 0:size] = jnp.zeros((size, size), BF16)

    @pl.when(mode == 1)
    def _():
        out_ref[0:half] = factor[:, 0:size]
        out_ref[half:tile] = factor[:, size : 2 * size]

    @pl.when(mode == 2)
    def _():
        update = dot(factor[...], rows_ref[...])
        out_ref[0:half] = (slab_ref[0:half].astype(F32) - update[:, 0:size]).astype(BF16)
        out_ref[half:tile] = (slab_ref[half:tile].astype(F32) - update[:, size : 2 * size]).astype(BF16)

        @pl.when(top & (own == 1))
        def _():
            base = slab_ref[0:size].astype(F32) + added_ref[...]
            out_ref[0:size] = (base - update[0:size, 0:size]).astype(BF16)


def panel(flags, token, lower, weights, rows, added, slab, parts, old, start, tile):
    size = slab.shape[1]
    offset = start // tile
    spans, begin, operands = [], 0, []
    for hops in parts:
        end = begin + hops[0].shape[0] // tile
        spans.append((begin, end))
        begin = end
        operands += hops
    blocks = [
        SMEM,
        ANY,
        pl.BlockSpec((size, size), lambda i: (0, 0)),
        pl.BlockSpec(weights.shape, lambda i: (0, 0)),
        pl.BlockSpec(rows.shape, lambda i: (0, 0)),
        pl.BlockSpec((size, size), lambda i: (0, 0)),
        pl.BlockSpec((tile, size), lambda i: (i + offset, 0)),
    ] + [ANY] * len(operands)
    pieces = len(operands)
    operands = [flags, token, lower, weights, rows, added, slab] + operands
    aliases = {}
    if old is not None:
        aliases = {len(operands): 0}
        blocks.append(ANY)
        operands.append(old)
    return pl.pallas_call(
        functools.partial(panel_kernel, pieces=range(pieces), spans=spans, first=start == 0),
        grid=(begin,),
        in_specs=blocks,
        out_specs=[pl.BlockSpec((tile, size), lambda i: (i + offset, 0)), SMEM],
        out_shape=[jax.ShapeDtypeStruct(slab.shape, BF16), jax.ShapeDtypeStruct((1,), jnp.int32)],
        input_output_aliases=aliases,
        scratch_shapes=[
            pltpu.VMEM((2, tile, size), BF16),
            pltpu.VMEM((tile // 2, 2 * size), BF16),
            pltpu.SemaphoreType.DMA((2,)),
        ],
        compiler_params=pltpu.CompilerParams(vmem_limit_bytes=16 * 2**20),
        cost_estimate=LIGHT,
        name="panel",
    )(*operands)


def broadcast(value, axis, source):
    kept = jnp.where(lax.axis_index(axis) == source, value, 0).astype(value.dtype)
    return lax.psum(kept, axis)


def settings(*values):
    return jnp.stack([jnp.asarray(value).astype(jnp.int32) for value in values])


def holder_pairs(wide, narrow, distance):
    stride = wide // narrow
    found = []
    for n in range(narrow):
        for start in range(0, wide, 2 * distance):
            source = (n * stride) ^ start
            found.append((source * narrow + n, (source ^ distance) * narrow + n))
    return found


class Order:
    def __init__(self, token):
        self.token = token

    def after(self, value):
        value, self.token = lax.optimization_barrier((value, self.token))
        return value


def known_owner(owner, coarse_basis, material_ids, lame_table, coarse_ids, coarse_slab):
    narrow, wide = lax.axis_size("narrow"), lax.axis_size("wide")
    stride = wide // narrow
    wide_index, narrow_index = lax.axis_index("wide"), lax.axis_index("narrow")
    height, block = coarse_slab.shape
    own = wide_index == narrow_index * stride
    later = narrow_index > owner
    which = jnp.where(later, narrow_index - owner - 1, -1)
    mode = jnp.where(narrow_index == owner, 1, jnp.where(later, 2, 0))
    earlier = (wide_index % stride == 0) & (wide_index // stride < owner)
    kind = jnp.where(wide_index == owner * stride, 1, jnp.where(earlier, 2, 0))
    table = lame_table.astype(F32)
    hops = narrow - 1 - owner
    units, joined, plan = PLANS[hops]
    unit = height // sum(units)
    count = len(units)
    bounds, low = [], 0
    for number in units:
        bounds.append((low, low + number * unit))
        low += number * unit
    axes = ("wide", "narrow")

    def rows_of(number):
        low, high = bounds[number]
        return coarse_slab[low:high]

    def send(value, source, target):
        return lax.ppermute(value, "narrow", [(owner + source, owner + target)])

    order = Order(settings(mode))

    ways = [((n * stride) * narrow + owner, (n * stride) * narrow + n) for n in range(owner + 1, narrow)]
    head = order.after(lax.ppermute(coarse_slab[:block], axes, ways))
    moved = {}

    groups = [[w for w in range(wide) if w % stride == 0], [w for w in range(wide) if w % stride]]
    groups = [group for group in groups if group]
    member = jnp.where(wide_index % stride == 0, 0, 1)

    def within(group, pairs):
        return [(w * narrow + one, w * narrow + two) for w in group for one, two in pairs]

    def halo_of(group, message):
        return lax.ppermute(message, axes, within(group, [(i + 1, i) for i in range(narrow - 1)]))

    spans = [bounds[0], (bounds[joined[0]][0], bounds[joined[-1]][1]) if joined else bounds[1]]
    first, last, *begun = halo_message(table, material_ids, order.token, coarse_basis, coarse_slab, spans)
    first = order.after(first)
    halos = [halo_of(groups[0], first)]
    moved[0] = [send(order.after(begun[0]), 0, hops)]
    edge = (narrow_index == 0).astype(jnp.int32).reshape(1)
    inner = order.after(interior(edge, table, material_ids, coarse_basis, order.token))
    if joined:
        whole = send(order.after(begun[1]), 0, 1)
    else:
        moved[1] = [send(order.after(begun[1]), 0, 1)]
    halos[0] = order.after(halos[0])
    for group in groups[1:]:
        halos.append(halo_of(group, order.after(first)))

    def nearest(base, extent):
        return min(range(base, min(base + extent, narrow)), key=lambda n: abs(n - owner))

    def summed(parts, distance, group):
        total = parts[0] if len(parts) == 1 else parts[0] + parts[1]
        pairs = []
        for base in range(0, narrow - distance, 2 * distance):
            one, two = nearest(base, distance), nearest(base + distance, distance)
            pairs.append((two, one) if nearest(base, 2 * distance) == one else (one, two))
        return [total, lax.ppermute(total, axes, within(group, pairs))], 2 * distance

    def faces_of(number):
        flag = settings(member == number)
        return [order.after(face(flag, table, material_ids, last, halos[number], order.token, inner))]

    sums, reach = [faces_of(0)], [1]
    while reach[0] < narrow:
        sums[0], reach[0] = summed(sums[0], reach[0], groups[0])
    sums[0][1] = order.after(sums[0][1])
    if not joined:
        for number in range(2, count - 1):
            moved[number] = [send(order.after(rows_of(number)), 0, 1)]
    distance, messages, left = wide // 2, [], plan.count("spread")
    result, prepared = None, None
    choice = (narrow_index - owner) % narrow
    flags = settings(mode, kind, own, which)
    for step in plan:
        if step[0] == "panel":
            if prepared is None:
                prepared = prepare(settings(choice, mode), order.token, head, summaries)
                added, galerkin = added_of(
                    settings(choice, mode, own), prepared[0], coarse_ids, galerkins, block
                )
            weights, rows, lower = prepared
            begin, end = step[1:]
            parts = [moved[number][:: 1 if number else -1] for number in range(begin, end)]
            result, order.token = panel(
                flags, order.token, lower, weights, rows, added if begin == 0 else head, coarse_slab, parts, result, bounds[begin][0], 2 * unit
            )
        elif step == "assemble":
            message = assemble(settings(mode, own), order.token, coarse_ids, coarse_slab, head, sums[0])
            message = order.after(message)
        elif step == "others":
            for number in range(1, len(groups)):
                halos[number] = order.after(halos[number])
                parts, far = summed(faces_of(number), 1, groups[number])
                sums.append(parts)
                reach.append(far)
        elif step == "more":
            for number in range(1, len(groups)):
                while reach[number] < narrow:
                    sums[number][1] = order.after(sums[number][1])
                    sums[number], reach[number] = summed(sums[number], reach[number], groups[number])
        elif step == "spread":
            left -= 1
            while distance:
                received = order.after(lax.ppermute(message, axes, holder_pairs(wide, narrow, distance)))
                messages = [message, received]
                if distance > 1:
                    message = message + received
                distance //= 2
                if left:
                    break
        elif step == "factor":
            summary, head, galerkin = factorize(settings(mode, member), order.token, messages, sums)
            summary = order.after(summary)
            ways = [[(owner, (owner + place) % narrow)] for place in range(1, narrow)]
            summaries = [summary] + [lax.ppermute(summary, "narrow", way) for way in ways]
            moved[count - 1] = [send(order.after(rows_of(count - 1)), 0, 1)]
            for place in range(1, narrow):
                summaries[place] = order.after(summaries[place])
            galerkin = order.after(galerkin)
            galerkins = [galerkin] + [lax.ppermute(galerkin, "narrow", way) for way in ways]
        else:
            number, hop = step
            if joined and step == (joined[0], 0):
                whole = order.after(whole)
                for part in joined:
                    low, high = (bound - bounds[joined[0]][0] for bound in bounds[part])
                    moved[part] = [whole[low:high]]
            moving = moved[number][hop] = order.after(moved[number][hop])
            if number == 0 and hop + 1 < hops:
                moved[number].append(send(moving, hops - hop, hops - hop - 1))
            elif number != 0 and hop + 1 < hops:
                moved[number].append(send(moving, hop + 1, hop + 2))
    return result, galerkin


def any_owner(owner, coarse_basis, material_ids, lame_table, coarse_ids, coarse_slab):
    narrow, wide = lax.axis_size("narrow"), lax.axis_size("wide")
    stride = wide // narrow
    wide_index, narrow_index = lax.axis_index("wide"), lax.axis_index("narrow")
    own = wide_index == narrow_index * stride
    later = narrow_index > owner
    which = jnp.where(later, 0, -1)
    mode = jnp.where(narrow_index == owner, 1, jnp.where(later, 2, 0))
    earlier = (wide_index % stride == 0) & (wide_index // stride < owner)
    kind = jnp.where(wide_index == owner * stride, 1, jnp.where(earlier, 2, 0))
    table = lame_table.astype(F32)
    column = broadcast(coarse_slab, "narrow", owner)
    first, last = halo_message(table, material_ids, table, coarse_basis, coarse_slab, ())
    halo = lax.ppermute(first, "narrow", [(i + 1, i) for i in range(narrow - 1)])
    edge = (narrow_index == 0).astype(jnp.int32).reshape(1)
    inner = interior(edge, table, material_ids, coarse_basis, first)
    partial = face(settings(1), table, material_ids, last, halo, first, inner)
    parts = [lax.psum(partial, "narrow")]
    message = assemble(settings(mode, own), first, coarse_ids, coarse_slab, column, parts)
    at_owner = (wide_index == owner * stride) & (narrow_index == owner)
    diagonal = lax.psum(jnp.where(at_owner, message, 0.0), ("wide", "narrow"))
    summary, _, galerkin = factorize(settings(1, 0), first, [diagonal], [parts])
    head = broadcast(message, "wide", narrow_index * stride)
    weights, rows, lower = prepare(settings(0, mode), settings(mode), head, [summary])
    added, galerkin = added_of(settings(0, mode, own), weights, coarse_ids, [galerkin], head.shape[0])
    flags = settings(mode, kind, own, which)
    tile = coarse_slab.shape[0] // 12
    result, _ = panel(flags, flags, lower, weights, rows, added, coarse_slab, [[column]], None, 0, tile)
    return result, galerkin


def on_device(coarse_basis, material_ids, lame_table, coarse_ids, coarse_slab, panel_owner):
    narrow, wide = lax.axis_size("narrow"), lax.axis_size("wide")
    arrays = (coarse_basis, material_ids, lame_table, coarse_ids, coarse_slab)
    owner = panel_owner[0]
    if narrow - 1 > len(PLANS) or wide & (wide - 1):
        return any_owner(owner, *arrays)
    branches = [functools.partial(known_owner, place) for place in range(narrow - 1)]
    return lax.switch(owner, branches, *arrays)


def solution(mesh):
    return jax.shard_map(
        on_device,
        mesh=mesh,
        in_specs=(
            P("wide", None, None, "narrow", None, None),
            P("wide", "narrow", None, None),
            P(),
            P("wide", None),
            P("wide", "narrow"),
            P(),
        ),
        out_specs=(P("wide", "narrow"), P("wide", None, None)),
        check_vma=False,
    )
```

profile of v0, /device:TPU:21, one launch (start us, length us, event | category | flops | bytes accessed | tf_op | source)
XLA Modules:
  0.0 146.0 jit_solution(9902455889546639484)
XLA Ops:
  1.3 144.5 %conditional.1 = (bf16[12288,128]{1,0:T(8,128)(2,1)}, f32[2,96,96]{2,1,0:T(8,128)}) conditional(s32[]{:T(128)} %bitcast.33, (bf16[12288,128]{1,0:T(8,128)(2,1)}, bf16[2,16]{1,0:T(2,128)(2,1)}, s32[2,4,8,128]{3,2,1,0:T(8,128)}, bf16[2,96,3,4,8,128]{5,4,3,2,1,0:T(8,128)(2,1)}, s32[2,96]{1,0:T(2,128)}) %tuple.102, ...), branch_computations={%region_0.1_spmd, %region_1.2_spmd, %region_2.3_spmd} | conditional | flops 69758 | bytes 103046432 | solution.py:810
  1.3 0.8 slice.26
  3.4 5.8 %halo_message.4 = (bf16[2,290,8,128]{3,2,1,0:T(8,128)(2,1)}, bf16[2,288,8,128]{3,2,1,0:T(8,128)(2,1)S(1)}, bf16[6144,128]{1,0:T(8,128)(2,1)}, bf16[3072,128]{1,0:T(8,128)(2,1)}) custom-call(f32[2,16]{1,0:T(2,128)S(1)} %convert_element_type.2.table_ref, s32[2,4,8,128]{3,2,1,0:T(8,128)} %get-tuple-element.122.ids_ref, s32[1]{0:T(128)} %bitcast.11.token_ref, ...), custom_call_target="tpu_custom_call" | custom-call | flops 1 | bytes 1 | tf_op jit(solution)/shard_map/cond/branch_1_fun/halo_message/pallas_call | solution.py:89
  9.2 1.9 %collective-permute-start.3 = (bf16[2,290,8,128]{3,2,1,0:T(8,128)(2,1)}, bf16[2,290,8,128]{3,2,1,0:T(8,128)(2,1)}, u32[]{:S(2)}, u32[]{:S(2)}) collective-permute-start(bf16[2,290,8,128]{3,2,1,0:T(8,128)(2,1)} %get-tuple-element.151), channel_id=1, source_target_pairs={{1,0},{2,1},{3,2},{9,8},{10,9},{11,10},{17,16},{18,17},{19,18},{25... | collective-permute-start | bytes 3563528 | tf_op jit(solution)/shard_map/cond/branch_1_fun/ppermute | solution.py:667
  11.1 0.7 collective-permute-start.2
  11.9 10.7 %interior.4.inner_ref = f32[2,96,96]{2,1,0:T(8,128)S(1)} custom-call(s32[1]{0:T(128)} %bitcast.16.edge_ref, f32[2,16]{1,0:T(2,128)S(1)} %convert_element_type.2.table_ref, s32[2,4,8,128]{3,2,1,0:T(8,128)S(1)} %copy-done.36, bf16[2,96,3,4,8,128]{5,4,3,2,1,0:T(8,128)(2,1)} %get-tuple-element.124.basis_ref, s32[1]{0:T(128)} %bitcast.11.token_ref), custom_call_target="tpu_custom_call" | custom-call | flops 1 | bytes 1 | tf_op jit(solution)/shard_map/cond/branch_1_fun/interior/pallas_call | solution.py:185
  22.6 5.6 %collective-permute-start.8 = (bf16[2,290,8,128]{3,2,1,0:T(8,128)(2,1)}, bf16[2,290,8,128]{3,2,1,0:T(8,128)(2,1)}, u32[]{:S(2)}, u32[]{:S(2)}) collective-permute-start(bf16[2,290,8,128]{3,2,1,0:T(8,128)(2,1)} %get-tuple-element.151), channel_id=1, source_target_pairs={{5,4},{6,5},{7,6},{13,12},{14,13},{15,14},{21,20},{22,21},{23,22},... | collective-permute-start | bytes 3563528 | tf_op jit(solution)/shard_map/cond/branch_1_fun/ppermute | solution.py:667
  28.3 1.3 collective-permute-start.1
  30.2 0.7 collective-permute-start.4
  30.9 0.7 collective-permute-start.5
  31.6 1.1 slice.27
  33.3 1.3 collective-permute-start.22
  34.6 0.8 copy.18.column_ids_ref
  36.0 1.7 %assemble.4 = f32[128,128]{1,0:T(8,128)} custom-call(s32[2]{0:T(128)} %pad_add_fusion.7.flags_ref, s32[1]{0:T(128)} %bitcast.11.token_ref, s32[2,96,1]{2,1,0:T(8,128)} %copy.18.column_ids_ref, s32[2,1,96]{2,1,0:T(1,128)S(1)} %bitcast.38, bf16[12288,128]{1,0:T(8,128)(2,1)} %get-tuple-element.120.slab_ref, bf16[128,128]{1,0:T(8,128)(2,1)} %copy-done.71, ...), custom_call_target="tpu_custom_call" | custom-call | flops 1 | bytes 1 | tf_op jit(solution)/shard_map/cond/branch_1_fun/assemble/pallas_call | solution.py:320
  38.3 0.9 add.60
  39.2 1.3 collective-permute-start.7
  40.4 4.5 %collective-permute-done.8.halo_ref = bf16[2,290,8,128]{3,2,1,0:T(8,128)(2,1)} collective-permute-done((bf16[2,290,8,128]{3,2,1,0:T(8,128)(2,1)}, bf16[2,290,8,128]{3,2,1,0:T(8,128)(2,1)}, u32[]{:S(2)}, u32[]{:S(2)}) %collective-permute-start.8) | collective-permute-done | bytes 1187872 | tf_op jit(solution)/shard_map/cond/branch_1_fun/ppermute | solution.py:667
  44.9 5.5 %face.9 = f32[2,96,96]{2,1,0:T(8,128)S(1)} custom-call(s32[1]{0:T(128)} %bitcast.20.flags_ref, f32[2,16]{1,0:T(2,128)S(1)} %convert_element_type.2.table_ref, s32[2,4,8,128]{3,2,1,0:T(8,128)S(1)} %copy-done.36, bf16[2,288,8,128]{3,2,1,0:T(8,128)(2,1)S(1)} %get-tuple-element.133.last_ref, bf16[2,290,8,128]{3,2,1,0:T(8,128)(2,1)} %collective-permute-done.8.halo_ref, ...), custom_call_target="tpu_custom_call" | custom-call | flops 1 | bytes 1 | tf_op jit(solution)/shard_map/cond/branch_1_fun/face/pallas_call | solution.py:263
  50.4 1.3 collective-permute-start.10
  51.7 0.8 add.61.refs_0_
  52.6 1.3 collective-permute-start.9
  53.9 1.3 collective-permute-start.13
  55.2 11.0 %collective-permute-done.10 = f32[2,96,96]{2,1,0:T(8,128)S(1)} collective-permute-done((f32[2,96,96]{2,1,0:T(8,128)S(1)}, f32[2,96,96]{2,1,0:T(8,128)S(1)}, u32[]{:S(2)}, u32[]{:S(2)}) %collective-permute-start.10) | collective-permute-done | bytes 73760 | tf_op jit(solution)/shard_map/cond/branch_1_fun/ppermute | solution.py:693
  66.2 9.6 %collective-permute-done.9.refs_1_ = f32[128,128]{1,0:T(8,128)S(1)} collective-permute-done((f32[128,128]{1,0:T(8,128)S(1)}, f32[128,128]{1,0:T(8,128)S(1)}, u32[]{:S(2)}, u32[]{:S(2)}) %collective-permute-start.9) | collective-permute-done | bytes 65568 | tf_op jit(solution)/shard_map/cond/branch_1_fun/ppermute | solution.py:740
  76.4 7.4 %collective-permute-start.17 = (bf16[3072,128]{1,0:T(8,128)(2,1)}, bf16[3072,128]{1,0:T(8,128)(2,1)S(1)}, u32[]{:S(2)}, u32[]{:S(2)}) collective-permute-start(bf16[3072,128]{1,0:T(8,128)(2,1)} %collective-permute-done.1.rest_0_), channel_id=1, source_target_pairs={{2,3},{6,7},{10,11},{14,15},{18,19},{22,23},{26,27},{30,31}} | collective-permute-start | bytes 2359304 | tf_op jit(solution)/shard_map/cond/branch_1_fun/ppermute | solution.py:651
  83.9 3.3 %collective-permute-start.11 = (f32[2,96,96]{2,1,0:T(8,128)S(1)}, f32[2,96,96]{2,1,0:T(8,128)}, u32[]{:S(2)}, u32[]{:S(2)}) collective-permute-start(f32[2,96,96]{2,1,0:T(8,128)S(1)} %add.62.refs_4_), channel_id=1, source_target_pairs={{6,5},{14,13},{22,21},{30,29}} | collective-permute-start | bytes 221192 | tf_op jit(solution)/shard_map/cond/branch_1_fun/ppermute | solution.py:693
  88.2 1.8 %factorize.4 = (bf16[384,128]{1,0:T(8,128)(2,1)}, f32[128,128]{1,0:T(8,128)}, f32[2,96,96]{2,1,0:T(8,128)}) custom-call(s32[2]{0:T(128)} %pad_add_fusion.6.flags_ref, s32[1]{0:T(128)} %bitcast.11.token_ref, f32[128,128]{1,0:T(8,128)} %copy-done.49, f32[128,128]{1,0:T(8,128)} %copy-done.68, f32[2,96,96]{2,1,0:T(8,128)} %copy-done.39, ...), custom_call_target="tpu_custom_call" | custom-call | flops 1 | bytes 1 | tf_op jit(solution)/shard_map/cond/branch_1_fun/factorize/pallas_call | solution.py:392
  90.0 1.3 collective-permute-start.16
  91.3 0.7 collective-permute-start.15
  92.0 8.0 %collective-permute-done.16.rest_1_ = bf16[384,128]{1,0:T(8,128)(2,1)S(1)} collective-permute-done((bf16[384,128]{1,0:T(8,128)(2,1)}, bf16[384,128]{1,0:T(8,128)(2,1)S(1)}, u32[]{:S(2)}, u32[]{:S(2)}) %collective-permute-start.16) | collective-permute-done | bytes 98336 | tf_op jit(solution)/shard_map/cond/branch_1_fun/ppermute | solution.py:751
  100.6 1.7 %slice.25 = bf16[1024,128]{1,0:T(8,128)(2,1)} slice(bf16[12288,128]{1,0:T(8,128)(2,1)} %get-tuple-element.120.slab_ref), slice={[11264:12288], [0:128]} | slice | bytes 524288 | tf_op jit(solution)/shard_map/cond/branch_1_fun/slice | solution.py:648
  103.6 2.9 %collective-permute-start.18 = (bf16[2048,128]{1,0:T(8,128)(2,1)S(1)}, bf16[2048,128]{1,0:T(8,128)(2,1)}, u32[]{:S(2)}, u32[]{:S(2)}) collective-permute-start(bf16[2048,128]{1,0:T(8,128)(2,1)S(1)} %collective-permute-done.13.rest_0_), channel_id=1, source_target_pairs={{2,3},{6,7},{10,11},{14,15},{18,19},{22,23},{26,27},{30,31}} | collective-permute-start | bytes 1572872 | tf_op jit(solution)/shard_map/cond/branch_1_fun/ppermute | solution.py:651
  106.6 1.3 collective-permute-start.12
  108.1 0.8 copy-done.10
  108.9 0.9 copy-done.21
  109.8 0.9 copy-done.23
  110.7 0.9 copy-done.26
  111.6 1.0 prepare.4
  112.6 5.0 %panel.15 = (bf16[12288,128]{1,0:T(8,128)(2,1)}, s32[1]{0:T(128)}) custom-call(s32[4]{0:T(128)S(1)} %pad_add_fusion.5.flags_ref, s32[1]{0:T(128)} %bitcast.11.token_ref, bf16[128,128]{1,0:T(8,128)(2,1)S(1)} %get-tuple-element.180.lower_ref, bf16[512,256]{1,0:T(8,128)(2,1)S(1)} %get-tuple-element.181.weights_ref.token_ref, ...), custom_call_target="tpu_custom_call" | custom-call | flops 1 | bytes 1 | tf_op jit(solution)/shard_map/cond/branch_1_fun/panel/pallas_call | solution.py:578
  117.7 1.3 collective-permute-start.23
  119.0 1.3 collective-permute-start.19
  120.3 0.7 collective-permute-start.20
  121.0 4.4 %collective-permute-done.19.rest_1_ = f32[2,96,96]{2,1,0:T(8,128)S(1)} collective-permute-done((f32[2,96,96]{2,1,0:T(8,128)S(1)}, f32[2,96,96]{2,1,0:T(8,128)S(1)}, u32[]{:S(2)}, u32[]{:S(2)}) %collective-permute-start.19) | collective-permute-done | bytes 73760 | tf_op jit(solution)/shard_map/cond/branch_1_fun/ppermute | solution.py:756
  128.0 1.8 %added.4 = (f32[128,128]{1,0:T(8,128)}, f32[2,96,96]{2,1,0:T(8,128)}) custom-call(s32[3]{0:T(128)} %pad_add_fusion.9.flags_ref, bf16[512,256]{1,0:T(8,128)(2,1)} %copy-done.3, s32[2,96,1]{2,1,0:T(8,128)} %copy.18.column_ids_ref, s32[2,1,96]{2,1,0:T(1,128)S(1)} %bitcast.39, f32[2,96,96]{2,1,0:T(8,128)} %get-tuple-element.189.rest_0_, ...), custom_call_target="tpu_custom_call" | custom-call | flops 1 | bytes 1 | tf_op jit(solution)/shard_map/cond/branch_1_fun/added/pallas_call | solution.py:470
  129.8 0.9 copy-done.4
  130.7 4.0 %panel.16 = (bf16[12288,128]{1,0:T(8,128)(2,1)}, s32[1]{0:T(128)}) custom-call(s32[4]{0:T(128)S(1)} %pad_add_fusion.5.flags_ref, s32[1]{0:T(128)} %get-tuple-element.185.token_ref, bf16[128,128]{1,0:T(8,128)(2,1)S(1)} %get-tuple-element.180.lower_ref, bf16[512,256]{1,0:T(8,128)(2,1)S(1)} %copy-done.4, ...), custom_call_target="tpu_custom_call", output_to_operand_aliasing={{0}: (9, {})} | custom-call | flops 1 | bytes 1 | tf_op jit(solution)/shard_map/cond/branch_1_fun/panel/pallas_call | solution.py:578
  134.7 7.2 %panel.17 = (bf16[12288,128]{1,0:T(8,128)(2,1)}, s32[1]{0:T(128)}) custom-call(s32[4]{0:T(128)S(1)} %pad_add_fusion.5.flags_ref, s32[1]{0:T(128)} %get-tuple-element.188.token_ref, bf16[128,128]{1,0:T(8,128)(2,1)S(1)} %get-tuple-element.180.lower_ref, bf16[512,256]{1,0:T(8,128)(2,1)S(1)} %copy-done.5, ...), custom_call_target="tpu_custom_call", output_to_operand_aliasing={{0}: (9, {})} | custom-call | flops 1 | bytes 1 | tf_op jit(solution)/shard_map/cond/branch_1_fun/panel/pallas_call | solution.py:578
  142.0 3.3 %panel.18 = (bf16[12288,128]{1,0:T(8,128)(2,1)}, s32[1]{0:T(128)}) custom-call(s32[4]{0:T(128)S(1)} %pad_add_fusion.5.flags_ref, s32[1]{0:T(128)} %get-tuple-element.193.token_ref, bf16[128,128]{1,0:T(8,128)(2,1)S(1)} %get-tuple-element.180.lower_ref, bf16[512,256]{1,0:T(8,128)(2,1)S(1)} %copy-done.5, ...), custom_call_target="tpu_custom_call", output_to_operand_aliasing={{0}: (9, {})} | custom-call | flops 1 | bytes 1 | tf_op jit(solution)/shard_map/cond/branch_1_fun/panel/pallas_call | solution.py:578
  (75 shorter events, 10.1 us)
Async XLA Ops:
  2.1 1.3 collective-permute-start
  3.4 5.8 %copy-start.71 = (bf16[128,128]{1,0:T(8,128)(2,1)}, bf16[128,128]{1,0:T(8,128)(2,1)S(1)}, u32[]{:S(2)}) copy-start(bf16[128,128]{1,0:T(8,128)(2,1)S(1)} %collective-permute-done.head_ref) | copy-start | bytes 98308 | tf_op jit(solution)/shard_map/cond
  3.4 8.5 %copy-start.36 = (s32[2,4,8,128]{3,2,1,0:T(8,128)S(1)}, s32[2,4,8,128]{3,2,1,0:T(8,128)}, u32[]{:S(2)}) copy-start(s32[2,4,8,128]{3,2,1,0:T(8,128)} %get-tuple-element.122.ids_ref) | copy-start | bytes 98308 | tf_op jit(solution)/shard_map/cond
  9.2 13.4 %collective-permute-start.3 = (bf16[2,290,8,128]{3,2,1,0:T(8,128)(2,1)}, bf16[2,290,8,128]{3,2,1,0:T(8,128)(2,1)}, u32[]{:S(2)}, u32[]{:S(2)}) collective-permute-start(bf16[2,290,8,128]{3,2,1,0:T(8,128)(2,1)} %get-tuple-element.151), channel_id=1, source_target_pairs={{1,0},{2,1},{3,2},{9,8},{10,9},{11,10},{17,16},{18,17},{19,18},{25... | collective-permute-start | bytes 3563528 | tf_op jit(solution)/shard_map/cond/branch_1_fun/ppermute | solution.py:667
  11.1 21.6 %collective-permute-start.2 = (bf16[6144,128]{1,0:T(8,128)(2,1)}, bf16[6144,128]{1,0:T(8,128)(2,1)S(1)}, u32[]{:S(2)}, u32[]{:S(2)}) collective-permute-start(bf16[6144,128]{1,0:T(8,128)(2,1)} %get-tuple-element.132), channel_id=1, source_target_pairs={{1,3},{5,7},{9,11},{13,15},{17,19},{21,23},{25,27},{29,31}} | collective-permute-start | bytes 4718600 | tf_op jit(solution)/shard_map/cond/branch_1_fun/ppermute | solution.py:651
  22.6 22.3 %collective-permute-start.8 = (bf16[2,290,8,128]{3,2,1,0:T(8,128)(2,1)}, bf16[2,290,8,128]{3,2,1,0:T(8,128)(2,1)}, u32[]{:S(2)}, u32[]{:S(2)}) collective-permute-start(bf16[2,290,8,128]{3,2,1,0:T(8,128)(2,1)} %get-tuple-element.151), channel_id=1, source_target_pairs={{5,4},{6,5},{7,6},{13,12},{14,13},{15,14},{21,20},{22,21},{23,22},... | collective-permute-start | bytes 3563528 | tf_op jit(solution)/shard_map/cond/branch_1_fun/ppermute | solution.py:667
  28.3 48.2 %collective-permute-start.1 = (bf16[3072,128]{1,0:T(8,128)(2,1)}, bf16[3072,128]{1,0:T(8,128)(2,1)}, u32[]{:S(2)}, u32[]{:S(2)}) collective-permute-start(bf16[3072,128]{1,0:T(8,128)(2,1)} %get-tuple-element.131), channel_id=1, source_target_pairs={{1,2},{5,6},{9,10},{13,14},{17,18},{21,22},{25,26},{29,30}} | collective-permute-start | bytes 2359304 | tf_op jit(solution)/shard_map/cond/branch_1_fun/ppermute | solution.py:651
  29.6 5.0 %copy-start.66 = (s32[2,96]{1,0:T(2,128)S(1)}, s32[2,96]{1,0:T(2,128)}, u32[]{:S(2)}) copy-start(s32[2,96]{1,0:T(2,128)} %get-tuple-element.145) | copy-start | bytes 2308 | tf_op jit(solution)/shard_map/cond
  30.2 0.7 collective-permute-start.4
  30.9 5.1 %copy-start.39 = (f32[2,96,96]{2,1,0:T(8,128)}, f32[2,96,96]{2,1,0:T(8,128)S(1)}, u32[]{:S(2)}) copy-start(f32[2,96,96]{2,1,0:T(8,128)S(1)} %add.59.rest_0_.refs_2_) | copy-start | bytes 221188 | tf_op jit(solution)/shard_map/cond
  30.9 1.8 %collective-permute-start.5 = (f32[2,96,96]{2,1,0:T(8,128)S(1)}, f32[2,96,96]{2,1,0:T(8,128)S(1)}, u32[]{:S(2)}, u32[]{:S(2)}) collective-permute-start(f32[2,96,96]{2,1,0:T(8,128)S(1)} %add.59.rest_0_.refs_2_), channel_id=1, source_target_pairs={{2,1},{10,9},{18,17},{26,25}} | collective-permute-start | bytes 221192 | tf_op jit(solution)/shard_map/cond/branch_1_fun/ppermute | solution.py:693
  32.7 0.6 copy-start.42
  33.3 101.4 %collective-permute-start.22 = (bf16[6144,128]{1,0:T(8,128)(2,1)S(1)}, bf16[6144,128]{1,0:T(8,128)(2,1)}, u32[]{:S(2)}, u32[]{:S(2)}) collective-permute-start(bf16[6144,128]{1,0:T(8,128)(2,1)S(1)} %collective-permute-done.2.rest_1_), channel_id=1, source_target_pairs={{3,2},{7,6},{11,10},{15,14},{19,18},{23,22},{27,26},{31,30}} | collective-permute-start | bytes 4718600 | tf_op jit(solution)/shard_map/cond/branch_1_fun/ppermute | solution.py:651
  37.6 0.7 collective-permute-start.6
  39.2 12.5 %collective-permute-start.7 = (f32[128,128]{1,0:T(8,128)S(1)}, f32[128,128]{1,0:T(8,128)}, u32[]{:S(2)}, u32[]{:S(2)}) collective-permute-start(f32[128,128]{1,0:T(8,128)S(1)} %add.60), channel_id=1, source_target_pairs={{0,8},{16,24},{9,1},{25,17},{18,26},{2,10},{27,19},{11,3}} | collective-permute-start | bytes 196616 | tf_op jit(solution)/shard_map/cond/branch_1_fun/ppermute | solution.py:740
  50.4 15.8 %collective-permute-start.10 = (f32[2,96,96]{2,1,0:T(8,128)S(1)}, f32[2,96,96]{2,1,0:T(8,128)S(1)}, u32[]{:S(2)}, u32[]{:S(2)}) collective-permute-start(f32[2,96,96]{2,1,0:T(8,128)S(1)} %face.9), channel_id=1, source_target_pairs={{4,5},{7,6},{12,13},{15,14},{20,21},{23,22},{28,29},{31,30}} | collective-permute-start | bytes 221192 | tf_op jit(solution)/shard_map/cond/branch_1_fun/ppermute | solution.py:693
  52.6 23.2 %copy-start.49 = (f32[128,128]{1,0:T(8,128)}, f32[128,128]{1,0:T(8,128)S(1)}, u32[]{:S(2)}) copy-start(f32[128,128]{1,0:T(8,128)S(1)} %add.61.refs_0_) | copy-start | bytes 196612 | tf_op jit(solution)/shard_map/cond
  52.6 23.2 %collective-permute-start.9 = (f32[128,128]{1,0:T(8,128)S(1)}, f32[128,128]{1,0:T(8,128)S(1)}, u32[]{:S(2)}, u32[]{:S(2)}) collective-permute-start(f32[128,128]{1,0:T(8,128)S(1)} %add.61.refs_0_), channel_id=1, source_target_pairs={{0,4},{8,12},{16,20},{24,28},{9,13},{1,5},{25,29},{17,21},{18,22},... | collective-permute-start | bytes 196616 | tf_op jit(solution)/shard_map/cond/branch_1_fun/ppermute | solution.py:740
  53.9 49.7 %collective-permute-start.13 = (bf16[2048,128]{1,0:T(8,128)(2,1)S(1)}, bf16[2048,128]{1,0:T(8,128)(2,1)S(1)}, u32[]{:S(2)}, u32[]{:S(2)}) collective-permute-start(bf16[2048,128]{1,0:T(8,128)(2,1)S(1)} %slice.27), channel_id=1, source_target_pairs={{1,2},{5,6},{9,10},{13,14},{17,18},{21,22},{25,26},{29,30}} | collective-permute-start | bytes 1572872 | tf_op jit(solution)/shard_map/cond/branch_1_fun/ppermute | solution.py:651
  75.8 0.6 copy-start.68
  76.4 36.2 %collective-permute-start.17 = (bf16[3072,128]{1,0:T(8,128)(2,1)}, bf16[3072,128]{1,0:T(8,128)(2,1)S(1)}, u32[]{:S(2)}, u32[]{:S(2)}) collective-permute-start(bf16[3072,128]{1,0:T(8,128)(2,1)} %collective-permute-done.1.rest_0_), channel_id=1, source_target_pairs={{2,3},{6,7},{10,11},{14,15},{18,19},{22,23},{26,27},{30,31}} | collective-permute-start | bytes 2359304 | tf_op jit(solution)/shard_map/cond/branch_1_fun/ppermute | solution.py:651
  83.9 4.3 %copy-start.46 = (f32[2,96,96]{2,1,0:T(8,128)}, f32[2,96,96]{2,1,0:T(8,128)S(1)}, u32[]{:S(2)}) copy-start(f32[2,96,96]{2,1,0:T(8,128)S(1)} %add.62.refs_4_) | copy-start | bytes 221188 | tf_op jit(solution)/shard_map/cond
  83.9 4.3 %collective-permute-start.11 = (f32[2,96,96]{2,1,0:T(8,128)S(1)}, f32[2,96,96]{2,1,0:T(8,128)}, u32[]{:S(2)}, u32[]{:S(2)}) collective-permute-start(f32[2,96,96]{2,1,0:T(8,128)S(1)} %add.62.refs_4_), channel_id=1, source_target_pairs={{6,5},{14,13},{22,21},{30,29}} | collective-permute-start | bytes 221192 | tf_op jit(solution)/shard_map/cond/branch_1_fun/ppermute | solution.py:693
  90.0 10.0 %collective-permute-start.16 = (bf16[384,128]{1,0:T(8,128)(2,1)}, bf16[384,128]{1,0:T(8,128)(2,1)S(1)}, u32[]{:S(2)}, u32[]{:S(2)}) collective-permute-start(bf16[384,128]{1,0:T(8,128)(2,1)} %get-tuple-element.169.rest_0_), channel_id=1, source_target_pairs={{1,2},{5,6},{9,10},{13,14},{17,18},{21,22},{25,26},{29,30}} | collective-permute-start | bytes 294920 | tf_op jit(solution)/shard_map/cond/branch_1_fun/ppermute | solution.py:751
  91.3 11.0 %collective-permute-start.15 = (bf16[384,128]{1,0:T(8,128)(2,1)}, bf16[384,128]{1,0:T(8,128)(2,1)S(1)}, u32[]{:S(2)}, u32[]{:S(2)}) collective-permute-start(bf16[384,128]{1,0:T(8,128)(2,1)} %get-tuple-element.169.rest_0_), channel_id=1, source_target_pairs={{1,3},{5,7},{9,11},{13,15},{17,19},{21,23},{25,27},{29,31}} | collective-permute-start | bytes 294920 | tf_op jit(solution)/shard_map/cond/branch_1_fun/ppermute | solution.py:751
  100.0 3.0 %collective-permute-start.14 = (bf16[384,128]{1,0:T(8,128)(2,1)}, bf16[384,128]{1,0:T(8,128)(2,1)S(1)}, u32[]{:S(2)}, u32[]{:S(2)}) collective-permute-start(bf16[384,128]{1,0:T(8,128)(2,1)} %get-tuple-element.169.rest_0_), channel_id=1, source_target_pairs={{1,0},{5,4},{9,8},{13,12},{17,16},{21,20},{25,24},{29,28}} | collective-permute-start | bytes 294920 | tf_op jit(solution)/shard_map/cond/branch_1_fun/ppermute | solution.py:751
  102.3 0.6 copy-start.22
  103.0 0.6 copy-start.25
  103.6 26.1 %collective-permute-start.18 = (bf16[2048,128]{1,0:T(8,128)(2,1)S(1)}, bf16[2048,128]{1,0:T(8,128)(2,1)}, u32[]{:S(2)}, u32[]{:S(2)}) collective-permute-start(bf16[2048,128]{1,0:T(8,128)(2,1)S(1)} %collective-permute-done.13.rest_0_), channel_id=1, source_target_pairs={{2,3},{6,7},{10,11},{14,15},{18,19},{22,23},{26,27},{30,31}} | collective-permute-start | bytes 1572872 | tf_op jit(solution)/shard_map/cond/branch_1_fun/ppermute | solution.py:651
  106.6 11.1 %collective-permute-start.12 = (bf16[1024,128]{1,0:T(8,128)(2,1)}, bf16[1024,128]{1,0:T(8,128)(2,1)}, u32[]{:S(2)}, u32[]{:S(2)}) collective-permute-start(bf16[1024,128]{1,0:T(8,128)(2,1)} %slice.25), channel_id=1, source_target_pairs={{1,2},{5,6},{9,10},{13,14},{17,18},{21,22},{25,26},{29,30}} | collective-permute-start | bytes 786440 | tf_op jit(solution)/shard_map/cond/branch_1_fun/ppermute | solution.py:651
  108.1 0.8 copy-start.10
  108.9 0.9 copy-start.21
  109.8 0.9 copy-start.23
  110.7 0.9 copy-start.26
  112.6 5.1 %copy-start.3 = (bf16[512,256]{1,0:T(8,128)(2,1)}, bf16[512,256]{1,0:T(8,128)(2,1)S(1)}, u32[]{:S(2)}) copy-start(bf16[512,256]{1,0:T(8,128)(2,1)S(1)} %get-tuple-element.181.weights_ref.token_ref) | copy-start | bytes 786436 | tf_op jit(solution)/shard_map/cond
  112.6 6.4 %copy-start.53 = (f32[2,96,96]{2,1,0:T(8,128)S(1)}, f32[2,96,96]{2,1,0:T(8,128)}, u32[]{:S(2)}) copy-start(f32[2,96,96]{2,1,0:T(8,128)} %get-tuple-element.189.rest_0_) | copy-start | bytes 221188 | tf_op jit(solution)/shard_map/cond
  112.6 17.1 %copy-start.11 = (f32[128,128]{1,0:T(8,128)S(1)}, f32[128,128]{1,0:T(8,128)}, u32[]{:S(2)}) copy-start(f32[128,128]{1,0:T(8,128)} %get-tuple-element.176.head_ref.added_ref) | copy-start | bytes 196612 | tf_op jit(solution)/shard_map/cond
  117.7 24.3 %collective-permute-start.23 = (bf16[1024,128]{1,0:T(8,128)(2,1)}, bf16[1024,128]{1,0:T(8,128)(2,1)S(1)}, u32[]{:S(2)}, u32[]{:S(2)}) collective-permute-start(bf16[1024,128]{1,0:T(8,128)(2,1)} %collective-permute-done.12.rest_0_), channel_id=1, source_target_pairs={{2,3},{6,7},{10,11},{14,15},{18,19},{22,23},{26,27},{30,31}} | collective-permute-start | bytes 786440 | tf_op jit(solution)/shard_map/cond/branch_1_fun/ppermute | solution.py:651
  119.0 6.4 %collective-permute-start.19 = (f32[2,96,96]{2,1,0:T(8,128)S(1)}, f32[2,96,96]{2,1,0:T(8,128)S(1)}, u32[]{:S(2)}, u32[]{:S(2)}) collective-permute-start(f32[2,96,96]{2,1,0:T(8,128)S(1)} %copy-done.53), channel_id=1, source_target_pairs={{1,2},{5,6},{9,10},{13,14},{17,18},{21,22},{25,26},{29,30}} | collective-permute-start | bytes 221192 | tf_op jit(solution)/shard_map/cond/branch_1_fun/ppermute | solution.py:756
  120.3 6.4 %collective-permute-start.20 = (f32[2,96,96]{2,1,0:T(8,128)S(1)}, f32[2,96,96]{2,1,0:T(8,128)S(1)}, u32[]{:S(2)}, u32[]{:S(2)}) collective-permute-start(f32[2,96,96]{2,1,0:T(8,128)S(1)} %copy-done.53), channel_id=1, source_target_pairs={{1,3},{5,7},{9,11},{13,15},{17,19},{21,23},{25,27},{29,31}} | collective-permute-start | bytes 221192 | tf_op jit(solution)/shard_map/cond/branch_1_fun/ppermute | solution.py:756
  125.4 1.3 copy-start.58
  125.4 1.3 collective-permute-start.21
  126.7 0.6 copy-start.60
  127.3 0.6 copy-start.63
  129.8 1.0 copy-start.4
  130.7 4.0 %copy-start.5 = (bf16[512,256]{1,0:T(8,128)(2,1)S(1)}, bf16[512,256]{1,0:T(8,128)(2,1)}, u32[]{:S(2)}) copy-start(bf16[512,256]{1,0:T(8,128)(2,1)} %copy-done.3) | copy-start | bytes 786436 | tf_op jit(solution)/shard_map/cond
  130.7 4.0 %copy-start.27 = (f32[128,128]{1,0:T(8,128)S(1)}, f32[128,128]{1,0:T(8,128)}, u32[]{:S(2)}) copy-start(f32[128,128]{1,0:T(8,128)} %get-tuple-element.190.added_ref) | copy-start | bytes 196612 | tf_op jit(solution)/shard_map/cond
  130.7 4.0 %copy-start.32 = (bf16[12288,128]{1,0:T(8,128)(2,1)S(1)}, bf16[12288,128]{1,0:T(8,128)(2,1)}, u32[]{:S(2)}) copy-start(bf16[12288,128]{1,0:T(8,128)(2,1)} %get-tuple-element.120.slab_ref) | copy-start | bytes 9437188 | tf_op jit(solution)/shard_map/cond
where the time goes:
time: 147 us; the launch traced here: 146 us
  Pallas kernels  48.4 us (33%)
  starting transfers between devices  40.1 us (27%)
  waiting for transfers between devices  37.9 us (26%)
  local copies, waits for them, and re-layouts  12.6 us (9%)
  other arithmetic  4.43 us (3%)
  between operations  1.48 us (1%)
    pallas_call x4, Pallas kernels, panel(): pl.pallas_call(functools.partial(panel_kernel, pieces=range(pieces), span...  19.5 us
    ppermute x8, starting transfers between devices, send(): return lax.ppermute(value, 'narrow', [(owner + source, owner + target)])  17.6 us
    ppermute x4, waiting for transfers between devices, summed(): lax.ppermute(total, axes, within(group, pairs))  11.4 us
    pallas_call x1, Pallas kernels, interior(): pl.pallas_call(interior_kernel, grid=(subs, comps), in_specs=[SMEM, SMEM,...  10.7 us
    ppermute x3, waiting for transfers between devices, known_owner(): lax.ppermute(message, axes, holder_pairs(wide, narrow, distance))  9.63 us
    cond x48, local copies, waits for them, and re-layouts  8.28 us
    ppermute x3, waiting for transfers between devices, known_owner(): lax.ppermute(summary, 'narrow', way)  8.01 us
    ppermute x2, starting transfers between devices, halo_of(): lax.ppermute(message, axes, within(group, [(i + 1, i) for i in range(narr...  7.5 us
  transfers between devices with their start and end apart: 24, of which 6 were waited for; matrix products, arithmetic and copies ran while one was open for 5% of the time, Pallas kernels for 27%

commit v1 on v0

--- a/solution.py
+++ b/solution.py
@@ -15,15 +15,18 @@
 SMEM = pl.BlockSpec(memory_space=pltpu.SMEM)
 PLANS = {
     1: (
-        (12, 10, 2),
+        (14, 8, 2),
         (),
-        ((0, 0), "assemble", "spread", "others", "spread", "more", "spread", "factor", ("panel", 1, 2), ("panel", 0, 1), ("panel", 2, 3)),
+        (
+            (0, 0), "assemble", "spread", "next", "others", "spread", "more", "spread", "factor",
+            ("panel", 1, 2), ("panel", 0, 1), ("panel", 2, 3),
+        ),
     ),
     2: (
-        (12, 6, 4, 2),
+        (14, 4, 4, 2),
         (),
         (
-            (0, 0), "assemble", "spread", "others", "spread", "more", "spread", (1, 0), "factor",
+            (0, 0), "next", "assemble", "spread", "others", "spread", "more", "spread", (1, 0), "factor",
             (2, 0), ("panel", 1, 2), (3, 0), ("panel", 2, 3), ("panel", 0, 1), ("panel", 3, 4),
         ),
     ),
@@ -31,7 +34,7 @@
         (12, 4, 4, 2, 2),
         (1, 2, 3),
         (
-            (0, 0), "assemble", "spread", "others", "spread", "more", "spread", "factor",
+            (0, 0), "next", "assemble", "spread", "others", "spread", "more", "spread", "factor",
             (1, 0), (1, 1), (0, 1), (2, 0), (2, 1), (3, 0), ("panel", 1, 2), (3, 1), (4, 0), ("panel", 2, 3), (4, 1),
             ("panel", 0, 1), ("panel", 3, 5),
         ),
@@ -673,10 +676,6 @@
     moved[0] = [send(order.after(begun[0]), 0, hops)]
     edge = (narrow_index == 0).astype(jnp.int32).reshape(1)
     inner = order.after(interior(edge, table, material_ids, coarse_basis, order.token))
-    if joined:
-        whole = send(order.after(begun[1]), 0, 1)
-    else:
-        moved[1] = [send(order.after(begun[1]), 0, 1)]
     halos[0] = order.after(halos[0])
     for group in groups[1:]:
         halos.append(halo_of(group, order.after(first)))
@@ -700,9 +699,6 @@
     while reach[0] < narrow:
         sums[0], reach[0] = summed(sums[0], reach[0], groups[0])
     sums[0][1] = order.after(sums[0][1])
-    if not joined:
-        for number in range(2, count - 1):
-            moved[number] = [send(order.after(rows_of(number)), 0, 1)]
     distance, messages, left = wide // 2, [], plan.count("spread")
     result, prepared = None, None
     choice = (narrow_index - owner) % narrow
@@ -720,6 +716,13 @@
             result, order.token = panel(
                 flags, order.token, lower, weights, rows, added if begin == 0 else head, coarse_slab, parts, result, bounds[begin][0], 2 * unit
             )
+        elif step == "next":
+            if joined:
+                whole = send(order.after(begun[1]), 0, 1)
+            else:
+                moved[1] = [send(order.after(begun[1]), 0, 1)]
+                for number in range(2, count - 1):
+                    moved[number] = [send(order.after(rows_of(number)), 0, 1)]
         elif step == "assemble":
             message = assemble(settings(mode, own), order.token, coarse_ids, coarse_slab, head, sums[0])
             message = order.after(message)

time: 147 us -> 187 us (1.27)
  the two profiles are of different devices: /device:TPU:21 before, /device:TPU:22 now
where the time goes in v1:
time: 187 us; the launch traced here: 183 us
  waiting for transfers between devices  73.1 us (39%)
  Pallas kernels  49.5 us (26%)
  starting transfers between devices  43.4 us (23%)
  local copies, waits for them, and re-layouts  11.9 us (6%)
  other arithmetic  2.79 us (1%)
    ppermute x13, waiting for transfers between devices, send(): return lax.ppermute(value, 'narrow', [(owner + source, owner + target)])  24.2 us
    pallas_call x4, Pallas kernels, panel(): pl.pallas_call(functools.partial(panel_kernel, pieces=range(pieces), span...  20.2 us
    ppermute x13, starting transfers between devices, send(): return lax.ppermute(value, 'narrow', [(owner + source, owner + target)])  20 us
    ppermute x2, waiting for transfers between devices, halo_of(): lax.ppermute(message, axes, within(group, [(i + 1, i) for i in range(narr...  18.2 us
    ppermute x3, waiting for transfers between devices, known_owner(): lax.ppermute(summary, 'narrow', way)  12.6 us
    pallas_call x1, Pallas kernels, interior(): pl.pallas_call(interior_kernel, grid=(subs, comps), in_specs=[SMEM, SMEM,...  10.7 us
    ppermute x4, starting transfers between devices, summed(): lax.ppermute(total, axes, within(group, pairs))  9.94 us
    ppermute x4, waiting for transfers between devices, summed(): lax.ppermute(total, axes, within(group, pairs))  8.53 us
  transfers between devices with their start and end apart: 29, of which 9 were waited for; matrix products, arithmetic and copies ran while one was open for 4% of the time, Pallas kernels for 21%

profile of v1, /device:TPU:22, one launch (start us, length us, event | category | flops | bytes accessed | tf_op | source)
XLA Modules:
  0.0 183.2 jit_solution(18356616462182602709)
XLA Ops:
  1.3 181.7 %conditional.1 = (bf16[12288,128]{1,0:T(8,128)(2,1)}, f32[2,96,96]{2,1,0:T(8,128)}) conditional(s32[]{:T(128)} %bitcast.33, (bf16[12288,128]{1,0:T(8,128)(2,1)}, bf16[2,16]{1,0:T(2,128)(2,1)}, s32[2,4,8,128]{3,2,1,0:T(8,128)}, bf16[2,96,3,4,8,128]{5,4,3,2,1,0:T(8,128)(2,1)}, s32[2,96]{1,0:T(2,128)}) %tuple.102, ...), branch_computations={%region_0.1_spmd, %region_1.2_spmd, %region_2.3_spmd} | conditional | flops 69758 | bytes 103046432 | solution.py:813
  3.4 6.2 %halo_message.3 = (bf16[2,290,8,128]{3,2,1,0:T(8,128)(2,1)}, bf16[2,288,8,128]{3,2,1,0:T(8,128)(2,1)S(1)}, bf16[6144,128]{1,0:T(8,128)(2,1)}, bf16[5120,128]{1,0:T(8,128)(2,1)}) custom-call(f32[2,16]{1,0:T(2,128)S(1)} %convert_element_type.0.table_ref, s32[2,4,8,128]{3,2,1,0:T(8,128)} %get-tuple-element.32.ids_ref, s32[1]{0:T(128)} %bitcast.token_ref, ...), custom_call_target="tpu_custom_call" | custom-call | flops 1 | bytes 1 | tf_op jit(solution)/shard_map/cond/branch_0_fun/halo_message/pallas_call | solution.py:92
  10.4 2.4 %collective-permute-start.45 = (bf16[2,290,8,128]{3,2,1,0:T(8,128)(2,1)}, bf16[2,290,8,128]{3,2,1,0:T(8,128)(2,1)}, u32[]{:S(2)}, u32[]{:S(2)}) collective-permute-start(bf16[2,290,8,128]{3,2,1,0:T(8,128)(2,1)} %get-tuple-element.59), channel_id=1, source_target_pairs={{1,0},{2,1},{3,2},{9,8},{10,9},{11,10},{17,16},{18,17},{19,18},{25... | collective-permute-start | bytes 3563528 | tf_op jit(solution)/shard_map/cond/branch_0_fun/ppermute | solution.py:670
  12.7 10.7 %interior.3.inner_ref = f32[2,96,96]{2,1,0:T(8,128)S(1)} custom-call(s32[1]{0:T(128)} %bitcast.6.edge_ref, f32[2,16]{1,0:T(2,128)S(1)} %convert_element_type.0.table_ref, s32[2,4,8,128]{3,2,1,0:T(8,128)S(1)} %copy-done.37, bf16[2,96,3,4,8,128]{5,4,3,2,1,0:T(8,128)(2,1)} %get-tuple-element.34.basis_ref, s32[1]{0:T(128)} %bitcast.token_ref), custom_call_target="tpu_custom_call" | custom-call | flops 1 | bytes 1 | tf_op jit(solution)/shard_map/cond/branch_0_fun/interior/pallas_call | solution.py:188
  23.5 18.2 %collective-permute-done.45.halo_ref = bf16[2,290,8,128]{3,2,1,0:T(8,128)(2,1)} collective-permute-done((bf16[2,290,8,128]{3,2,1,0:T(8,128)(2,1)}, bf16[2,290,8,128]{3,2,1,0:T(8,128)(2,1)}, u32[]{:S(2)}, u32[]{:S(2)}) %collective-permute-start.45) | collective-permute-done | bytes 1187872 | tf_op jit(solution)/shard_map/cond/branch_0_fun/ppermute | solution.py:670
  41.7 1.8 collective-permute-start.50
  43.5 5.5 %face.6 = f32[2,96,96]{2,1,0:T(8,128)S(1)} custom-call(s32[1]{0:T(128)} %bitcast.5.flags_ref, f32[2,16]{1,0:T(2,128)S(1)} %convert_element_type.0.table_ref, s32[2,4,8,128]{3,2,1,0:T(8,128)S(1)} %copy-done.37, bf16[2,288,8,128]{3,2,1,0:T(8,128)(2,1)S(1)} %get-tuple-element.40.last_ref, bf16[2,290,8,128]{3,2,1,0:T(8,128)(2,1)} %collective-permute-done.45.halo_ref, ...), custom_call_target="tpu_custom_call" | custom-call | flops 1 | bytes 1 | tf_op jit(solution)/shard_map/cond/branch_0_fun/face/pallas_call | solution.py:266
  49.0 1.3 collective-permute-start.46
  50.3 6.3 %collective-permute-done.46 = f32[2,96,96]{2,1,0:T(8,128)S(1)} collective-permute-done((f32[2,96,96]{2,1,0:T(8,128)S(1)}, f32[2,96,96]{2,1,0:T(8,128)S(1)}, u32[]{:S(2)}, u32[]{:S(2)}) %collective-permute-start.46) | collective-permute-done | bytes 73760 | tf_op jit(solution)/shard_map/cond/branch_0_fun/ppermute | solution.py:692
  56.6 7.3 %collective-permute-start.47 = (f32[2,96,96]{2,1,0:T(8,128)S(1)}, f32[2,96,96]{2,1,0:T(8,128)S(1)}, u32[]{:S(2)}, u32[]{:S(2)}) collective-permute-start(f32[2,96,96]{2,1,0:T(8,128)S(1)} %add.53.rest_0_.refs_2_), channel_id=1, source_target_pairs={{2,0},{10,8},{18,16},{26,24}} | collective-permute-start | bytes 221192 | tf_op jit(solution)/shard_map/cond/branch_0_fun/ppermute | solution.py:692
  64.0 2.2 %collective-permute-done.47.rest_1_.refs_3_ = f32[2,96,96]{2,1,0:T(8,128)S(1)} collective-permute-done((f32[2,96,96]{2,1,0:T(8,128)S(1)}, f32[2,96,96]{2,1,0:T(8,128)S(1)}, u32[]{:S(2)}, u32[]{:S(2)}) %collective-permute-start.47) | collective-permute-done | bytes 73760 | tf_op jit(solution)/shard_map/cond/branch_0_fun/ppermute | solution.py:692
  66.2 1.8 collective-permute-start.55
  67.9 1.3 collective-permute-start.59
  70.7 1.7 assemble.3
  74.4 1.3 collective-permute-start.49
  75.7 4.9 %collective-permute-done.49 = f32[128,128]{1,0:T(8,128)S(1)} collective-permute-done((f32[128,128]{1,0:T(8,128)S(1)}, f32[128,128]{1,0:T(8,128)S(1)}, u32[]{:S(2)}, u32[]{:S(2)}) %collective-permute-start.49) | collective-permute-done | bytes 65568 | tf_op jit(solution)/shard_map/cond/branch_0_fun/ppermute | solution.py:743
  80.6 1.3 collective-permute-start.51
  84.5 1.9 %factorize.3 = (bf16[384,128]{1,0:T(8,128)(2,1)}, f32[128,128]{1,0:T(8,128)}, f32[2,96,96]{2,1,0:T(8,128)}) custom-call(s32[2]{0:T(128)} %pad_add_fusion.1.flags_ref, s32[1]{0:T(128)} %bitcast.token_ref, f32[128,128]{1,0:T(8,128)} %copy-done.52, f32[128,128]{1,0:T(8,128)} %copy-done.72, f32[2,96,96]{2,1,0:T(8,128)} %copy-done.42, f32[2,96,96]{2,1,0:T(8,128)} %copy-done.45, ...), custom_call_target="tpu_custom_call" | custom-call | flops 1 | bytes 1 | tf_op jit(solution)/shard_map/cond/branch_0_fun/factorize/pallas_call | solution.py:395
  87.2 1.3 collective-permute-start.57
  89.2 1.0 slice.20
  90.2 12.6 %collective-permute-done.57.rest_2_ = bf16[384,128]{1,0:T(8,128)(2,1)S(1)} collective-permute-done((bf16[384,128]{1,0:T(8,128)(2,1)}, bf16[384,128]{1,0:T(8,128)(2,1)S(1)}, u32[]{:S(2)}, u32[]{:S(2)}) %collective-permute-start.57) | collective-permute-done | bytes 98336 | tf_op jit(solution)/shard_map/cond/branch_0_fun/ppermute | solution.py:754
  102.7 1.3 fusion
  104.1 1.3 collective-permute-start.60
  105.4 13.2 %collective-permute-done.60.rest_1_ = bf16[2048,128]{1,0:T(8,128)(2,1)} collective-permute-done((bf16[2048,128]{1,0:T(8,128)(2,1)S(1)}, bf16[2048,128]{1,0:T(8,128)(2,1)}, u32[]{:S(2)}, u32[]{:S(2)}) %collective-permute-start.60) | collective-permute-done | bytes 524320 | tf_op jit(solution)/shard_map/cond/branch_0_fun/ppermute | solution.py:654
  118.6 2.5 %collective-permute-start.69 = (bf16[6144,128]{1,0:T(8,128)(2,1)}, bf16[6144,128]{1,0:T(8,128)(2,1)}, u32[]{:S(2)}, u32[]{:S(2)}) collective-permute-start(bf16[6144,128]{1,0:T(8,128)(2,1)} %collective-permute-done.59.rest_1_), channel_id=1, source_target_pairs={{2,1},{6,5},{10,9},{14,13},{18,17},{22,21},{26,25},{30,29}} | collective-permute-start | bytes 4718600 | tf_op jit(solution)/shard_map/cond/branch_0_fun/ppermute | solution.py:654
  121.1 1.3 collective-permute-start.61
  122.4 2.2 %collective-permute-start.63 = (bf16[2048,128]{1,0:T(8,128)(2,1)}, bf16[2048,128]{1,0:T(8,128)(2,1)}, u32[]{:S(2)}, u32[]{:S(2)}) collective-permute-start(bf16[2048,128]{1,0:T(8,128)(2,1)} %collective-permute-done.60.rest_1_), channel_id=1, source_target_pairs={{2,3},{6,7},{10,11},{14,15},{18,19},{22,23},{26,27},{30,31}} | collective-permute-start | bytes 1572872 | tf_op jit(solution)/shard_map/cond/branch_0_fun/ppermute | solution.py:654
  124.6 1.0 slice.22.rest_0_
  125.5 9.0 %collective-permute-done.61.rest_1_ = bf16[2048,128]{1,0:T(8,128)(2,1)} collective-permute-done((bf16[2048,128]{1,0:T(8,128)(2,1)S(1)}, bf16[2048,128]{1,0:T(8,128)(2,1)}, u32[]{:S(2)}, u32[]{:S(2)}) %collective-permute-start.61) | collective-permute-done | bytes 524320 | tf_op jit(solution)/shard_map/cond/branch_0_fun/ppermute | solution.py:654
  134.6 1.3 collective-permute-start.62
  135.9 1.4 collective-permute-start.54
  137.2 2.1 %collective-permute-start.65 = (bf16[2048,128]{1,0:T(8,128)(2,1)}, bf16[2048,128]{1,0:T(8,128)(2,1)}, u32[]{:S(2)}, u32[]{:S(2)}) collective-permute-start(bf16[2048,128]{1,0:T(8,128)(2,1)} %collective-permute-done.61.rest_1_), channel_id=1, source_target_pairs={{2,3},{6,7},{10,11},{14,15},{18,19},{22,23},{26,27},{30,31}} | collective-permute-start | bytes 1572872 | tf_op jit(solution)/shard_map/cond/branch_0_fun/ppermute | solution.py:654
  139.5 0.9 copy-done.16
  140.4 0.9 copy-done.18
  141.3 0.9 copy-done.20
  142.2 1.0 prepare.3
  143.2 3.8 %panel.11 = (bf16[12288,128]{1,0:T(8,128)(2,1)S(1)}, s32[1]{0:T(128)}) custom-call(s32[4]{0:T(128)S(1)} %pad_add_fusion.flags_ref, s32[1]{0:T(128)} %bitcast.token_ref, bf16[128,128]{1,0:T(8,128)(2,1)S(1)} %get-tuple-element.98.lower_ref, bf16[512,256]{1,0:T(8,128)(2,1)S(1)} %get-tuple-element.99.weights_ref.token_ref, ...), custom_call_target="tpu_custom_call" | custom-call | flops 1 | bytes 1 | tf_op jit(solution)/shard_map/cond/branch_0_fun/panel/pallas_call | solution.py:581
  147.1 1.3 collective-permute-start.64
  148.4 1.3 collective-permute-start.70
  149.7 3.9 %panel.12 = (bf16[12288,128]{1,0:T(8,128)(2,1)S(1)}, s32[1]{0:T(128)}) custom-call(s32[4]{0:T(128)S(1)} %pad_add_fusion.flags_ref, s32[1]{0:T(128)} %get-tuple-element.105.token_ref, bf16[128,128]{1,0:T(8,128)(2,1)S(1)} %get-tuple-element.98.lower_ref, ...), custom_call_target="tpu_custom_call", output_to_operand_aliasing={{0}: (10, {})} | custom-call | flops 1 | bytes 1 | tf_op jit(solution)/shard_map/cond/branch_0_fun/panel/pallas_call | solution.py:581
  153.6 1.9 %collective-permute-done.64.rest_4_ = bf16[1024,128]{1,0:T(8,128)(2,1)S(1)} collective-permute-done((bf16[1024,128]{1,0:T(8,128)(2,1)}, bf16[1024,128]{1,0:T(8,128)(2,1)S(1)}, u32[]{:S(2)}, u32[]{:S(2)}) %collective-permute-start.64) | collective-permute-done | bytes 262176 | tf_op jit(solution)/shard_map/cond/branch_0_fun/ppermute | solution.py:654
  155.6 1.6 collective-permute-start.71
  157.9 1.3 collective-permute-start.67
  160.5 4.7 %collective-permute-done.67.rest_2_ = f32[2,96,96]{2,1,0:T(8,128)S(1)} collective-permute-done((f32[2,96,96]{2,1,0:T(8,128)S(1)}, f32[2,96,96]{2,1,0:T(8,128)S(1)}, u32[]{:S(2)}, u32[]{:S(2)}) %collective-permute-start.67) | collective-permute-done | bytes 73760 | tf_op jit(solution)/shard_map/cond/branch_0_fun/ppermute | solution.py:759
  166.5 1.8 added.3
  168.3 0.9 copy-done.1
  170.1 8.5 %panel.13 = (bf16[12288,128]{1,0:T(8,128)(2,1)}, s32[1]{0:T(128)}) custom-call(s32[4]{0:T(128)S(1)} %pad_add_fusion.flags_ref, s32[1]{0:T(128)} %get-tuple-element.109.token_ref, bf16[128,128]{1,0:T(8,128)(2,1)S(1)} %get-tuple-element.98.lower_ref, bf16[512,256]{1,0:T(8,128)(2,1)S(1)} %copy-done.1, ...), custom_call_target="tpu_custom_call", output_to_operand_aliasing={{0}: (10, {})} | custom-call | flops 1 | bytes 1 | tf_op jit(solution)/shard_map/cond/branch_0_fun/panel/pallas_call | solution.py:581
  178.7 4.0 %panel.14 = (bf16[12288,128]{1,0:T(8,128)(2,1)}, s32[1]{0:T(128)}) custom-call(s32[4]{0:T(128)S(1)} %pad_add_fusion.flags_ref, s32[1]{0:T(128)} %get-tuple-element.114.token_ref, bf16[128,128]{1,0:T(8,128)(2,1)S(1)} %get-tuple-element.98.lower_ref, bf16[512,256]{1,0:T(8,128)(2,1)S(1)} %copy-done.2, ...), custom_call_target="tpu_custom_call", output_to_operand_aliasing={{0}: (13, {})} | custom-call | flops 1 | bytes 1 | tf_op jit(solution)/shard_map/cond/branch_0_fun/panel/pallas_call | solution.py:581
  (96 shorter events, 14.7 us)
Async XLA Ops:
  2.1 1.3 collective-permute-start.43
  3.4 6.2 %copy-start.75 = (bf16[128,128]{1,0:T(8,128)(2,1)}, bf16[128,128]{1,0:T(8,128)(2,1)S(1)}, u32[]{:S(2)}) copy-start(bf16[128,128]{1,0:T(8,128)(2,1)S(1)} %collective-permute-done.43.head_ref) | copy-start | bytes 98308 | tf_op jit(solution)/shard_map/cond
  3.4 9.3 %copy-start.37 = (s32[2,4,8,128]{3,2,1,0:T(8,128)S(1)}, s32[2,4,8,128]{3,2,1,0:T(8,128)}, u32[]{:S(2)}) copy-start(s32[2,4,8,128]{3,2,1,0:T(8,128)} %get-tuple-element.32.ids_ref) | copy-start | bytes 98308 | tf_op jit(solution)/shard_map/cond
  9.6 56.6 %collective-permute-start.44 = (bf16[6144,128]{1,0:T(8,128)(2,1)}, bf16[6144,128]{1,0:T(8,128)(2,1)S(1)}, u32[]{:S(2)}, u32[]{:S(2)}) collective-permute-start(bf16[6144,128]{1,0:T(8,128)(2,1)} %get-tuple-element.39), channel_id=1, source_target_pairs={{0,3},{4,7},{8,11},{12,15},{16,19},{20,23},{24,27},{28,31}} | collective-permute-start | bytes 4718600 | tf_op jit(solution)/shard_map/cond/branch_0_fun/ppermute | solution.py:654
  10.4 31.4 %collective-permute-start.45 = (bf16[2,290,8,128]{3,2,1,0:T(8,128)(2,1)}, bf16[2,290,8,128]{3,2,1,0:T(8,128)(2,1)}, u32[]{:S(2)}, u32[]{:S(2)}) collective-permute-start(bf16[2,290,8,128]{3,2,1,0:T(8,128)(2,1)} %get-tuple-element.59), channel_id=1, source_target_pairs={{1,0},{2,1},{3,2},{9,8},{10,9},{11,10},{17,16},{18,17},{19,18},{25... | collective-permute-start | bytes 3563528 | tf_op jit(solution)/shard_map/cond/branch_0_fun/ppermute | solution.py:670
  23.5 45.8 %copy-start.68 = (s32[2,96]{1,0:T(2,128)S(1)}, s32[2,96]{1,0:T(2,128)}, u32[]{:S(2)}) copy-start(s32[2,96]{1,0:T(2,128)} %get-tuple-element.53) | copy-start | bytes 2308 | tf_op jit(solution)/shard_map/cond
  41.7 31.4 %collective-permute-start.50 = (bf16[2,290,8,128]{3,2,1,0:T(8,128)(2,1)}, bf16[2,290,8,128]{3,2,1,0:T(8,128)(2,1)}, u32[]{:S(2)}, u32[]{:S(2)}) collective-permute-start(bf16[2,290,8,128]{3,2,1,0:T(8,128)(2,1)} %get-tuple-element.59), channel_id=1, source_target_pairs={{5,4},{6,5},{7,6},{13,12},{14,13},{15,14},{21,20},{22,21},{23,22},... | collective-permute-start | bytes 3563528 | tf_op jit(solution)/shard_map/cond/branch_0_fun/ppermute | solution.py:670
  49.0 7.6 %collective-permute-start.46 = (f32[2,96,96]{2,1,0:T(8,128)S(1)}, f32[2,96,96]{2,1,0:T(8,128)S(1)}, u32[]{:S(2)}, u32[]{:S(2)}) collective-permute-start(f32[2,96,96]{2,1,0:T(8,128)S(1)} %face.6), channel_id=1, source_target_pairs={{1,0},{3,2},{9,8},{11,10},{17,16},{19,18},{25,24},{27,26}} | collective-permute-start | bytes 221192 | tf_op jit(solution)/shard_map/cond/branch_0_fun/ppermute | solution.py:692
  56.6 14.0 %copy-start.42 = (f32[2,96,96]{2,1,0:T(8,128)}, f32[2,96,96]{2,1,0:T(8,128)S(1)}, u32[]{:S(2)}) copy-start(f32[2,96,96]{2,1,0:T(8,128)S(1)} %add.53.rest_0_.refs_2_) | copy-start | bytes 221188 | tf_op jit(solution)/shard_map/cond
  56.6 9.5 %collective-permute-start.47 = (f32[2,96,96]{2,1,0:T(8,128)S(1)}, f32[2,96,96]{2,1,0:T(8,128)S(1)}, u32[]{:S(2)}, u32[]{:S(2)}) collective-permute-start(f32[2,96,96]{2,1,0:T(8,128)S(1)} %add.53.rest_0_.refs_2_), channel_id=1, source_target_pairs={{2,0},{10,8},{18,16},{26,24}} | collective-permute-start | bytes 221192 | tf_op jit(solution)/shard_map/cond/branch_0_fun/ppermute | solution.py:692
  66.2 4.5 %copy-start.45 = (f32[2,96,96]{2,1,0:T(8,128)}, f32[2,96,96]{2,1,0:T(8,128)S(1)}, u32[]{:S(2)}) copy-start(f32[2,96,96]{2,1,0:T(8,128)S(1)} %collective-permute-done.47.rest_1_.refs_3_) | copy-start | bytes 221188 | tf_op jit(solution)/shard_map/cond
  66.2 36.6 %collective-permute-start.55 = (bf16[5120,128]{1,0:T(8,128)(2,1)}, bf16[5120,128]{1,0:T(8,128)(2,1)}, u32[]{:S(2)}, u32[]{:S(2)}) collective-permute-start(bf16[5120,128]{1,0:T(8,128)(2,1)} %get-tuple-element.74), channel_id=1, source_target_pairs={{0,1},{4,5},{8,9},{12,13},{16,17},{20,21},{24,25},{28,29}} | collective-permute-start | bytes 3932168 | tf_op jit(solution)/shard_map/cond/branch_0_fun/ppermute | solution.py:654
  67.9 50.6 %collective-permute-start.59 = (bf16[6144,128]{1,0:T(8,128)(2,1)S(1)}, bf16[6144,128]{1,0:T(8,128)(2,1)}, u32[]{:S(2)}, u32[]{:S(2)}) collective-permute-start(bf16[6144,128]{1,0:T(8,128)(2,1)S(1)} %collective-permute-done.44.rest_2_), channel_id=1, source_target_pairs={{3,2},{7,6},{11,10},{15,14},{19,18},{23,22},{27,26},{31,30}} | collective-permute-start | bytes 4718600 | tf_op jit(solution)/shard_map/cond/branch_0_fun/ppermute | solution.py:654
  72.3 2.1 %copy-start.50 = (f32[128,128]{1,0:T(8,128)S(1)}, f32[128,128]{1,0:T(8,128)}, u32[]{:S(2)}) copy-start(f32[128,128]{1,0:T(8,128)} %assemble.3) | copy-start | bytes 196612 | tf_op jit(solution)/shard_map/cond
  72.3 0.8 collective-permute-start.48
  73.7 8.2 %collective-permute-start.52 = (f32[2,96,96]{2,1,0:T(8,128)S(1)}, f32[2,96,96]{2,1,0:T(8,128)S(1)}, u32[]{:S(2)}, u32[]{:S(2)}) collective-permute-start(f32[2,96,96]{2,1,0:T(8,128)S(1)} %face.7), channel_id=1, source_target_pairs={{5,4},{7,6},{13,12},{15,14},{21,20},{23,22},{29,28},{31,30}} | collective-permute-start | bytes 221192 | tf_op jit(solution)/shard_map/cond/branch_0_fun/ppermute | solution.py:692
  74.4 6.2 %collective-permute-start.49 = (f32[128,128]{1,0:T(8,128)S(1)}, f32[128,128]{1,0:T(8,128)S(1)}, u32[]{:S(2)}, u32[]{:S(2)}) collective-permute-start(f32[128,128]{1,0:T(8,128)S(1)} %add.54), channel_id=1, source_target_pairs={{0,8},{16,24},{9,1},{25,17},{18,26},{2,10},{27,19},{11,3}} | collective-permute-start | bytes 196616 | tf_op jit(solution)/shard_map/cond/branch_0_fun/ppermute | solution.py:743
  80.6 2.6 %copy-start.52 = (f32[128,128]{1,0:T(8,128)}, f32[128,128]{1,0:T(8,128)S(1)}, u32[]{:S(2)}) copy-start(f32[128,128]{1,0:T(8,128)S(1)} %add.55.refs_0_) | copy-start | bytes 196612 | tf_op jit(solution)/shard_map/cond
  80.6 2.6 %collective-permute-start.51 = (f32[128,128]{1,0:T(8,128)S(1)}, f32[128,128]{1,0:T(8,128)S(1)}, u32[]{:S(2)}, u32[]{:S(2)}) collective-permute-start(f32[128,128]{1,0:T(8,128)S(1)} %add.55.refs_0_), channel_id=1, source_target_pairs={{0,4},{8,12},{16,20},{24,28},{9,13},{1,5},{25,29},{17,21},{18,22},... | collective-permute-start | bytes 196616 | tf_op jit(solution)/shard_map/cond/branch_0_fun/ppermute | solution.py:743
  82.0 1.3 collective-permute-start.53
  86.4 53.1 %copy-start.9 = (f32[128,128]{1,0:T(8,128)S(1)}, f32[128,128]{1,0:T(8,128)}, u32[]{:S(2)}) copy-start(f32[128,128]{1,0:T(8,128)} %get-tuple-element.94.head_ref.added_ref) | copy-start | bytes 196612 | tf_op jit(solution)/shard_map/cond
  86.4 53.1 %copy-start.14 = (bf16[384,128]{1,0:T(8,128)(2,1)S(1)}, bf16[384,128]{1,0:T(8,128)(2,1)}, u32[]{:S(2)}) copy-start(bf16[384,128]{1,0:T(8,128)(2,1)} %get-tuple-element.76.rest_0_) | copy-start | bytes 294916 | tf_op jit(solution)/shard_map/cond
  86.4 3.7 %collective-permute-start.58 = (bf16[384,128]{1,0:T(8,128)(2,1)}, bf16[384,128]{1,0:T(8,128)(2,1)S(1)}, u32[]{:S(2)}, u32[]{:S(2)}) collective-permute-start(bf16[384,128]{1,0:T(8,128)(2,1)} %get-tuple-element.76.rest_0_), channel_id=1, source_target_pairs={{0,1},{4,5},{8,9},{12,13},{16,17},{20,21},{24,25},{28,29}} | collective-permute-start | bytes 294920 | tf_op jit(solution)/shard_map/cond/branch_0_fun/ppermute | solution.py:754
  87.2 15.5 %collective-permute-start.57 = (bf16[384,128]{1,0:T(8,128)(2,1)}, bf16[384,128]{1,0:T(8,128)(2,1)S(1)}, u32[]{:S(2)}, u32[]{:S(2)}) collective-permute-start(bf16[384,128]{1,0:T(8,128)(2,1)} %get-tuple-element.76.rest_0_), channel_id=1, source_target_pairs={{0,2},{4,6},{8,10},{12,14},{16,18},{20,22},{24,26},{28,30}} | collective-permute-start | bytes 294920 | tf_op jit(solution)/shard_map/cond/branch_0_fun/ppermute | solution.py:754
  88.5 14.2 %collective-permute-start.56 = (bf16[384,128]{1,0:T(8,128)(2,1)}, bf16[384,128]{1,0:T(8,128)(2,1)S(1)}, u32[]{:S(2)}, u32[]{:S(2)}) collective-permute-start(bf16[384,128]{1,0:T(8,128)(2,1)} %get-tuple-element.76.rest_0_), channel_id=1, source_target_pairs={{0,3},{4,7},{8,11},{12,15},{16,19},{20,23},{24,27},{28,31}} | collective-permute-start | bytes 294920 | tf_op jit(solution)/shard_map/cond/branch_0_fun/ppermute | solution.py:754
  90.2 32.2 %copy-start.15 = (bf16[384,128]{1,0:T(8,128)(2,1)}, bf16[384,128]{1,0:T(8,128)(2,1)S(1)}, u32[]{:S(2)}) copy-start(bf16[384,128]{1,0:T(8,128)(2,1)S(1)} %collective-permute-done.58.rest_1_) | copy-start | bytes 294916 | tf_op jit(solution)/shard_map/cond
  102.7 19.7 %copy-start.17 = (bf16[384,128]{1,0:T(8,128)(2,1)}, bf16[384,128]{1,0:T(8,128)(2,1)S(1)}, u32[]{:S(2)}) copy-start(bf16[384,128]{1,0:T(8,128)(2,1)S(1)} %collective-permute-done.57.rest_2_) | copy-start | bytes 294916 | tf_op jit(solution)/shard_map/cond
  102.7 19.7 %copy-start.19 = (bf16[384,128]{1,0:T(8,128)(2,1)}, bf16[384,128]{1,0:T(8,128)(2,1)S(1)}, u32[]{:S(2)}) copy-start(bf16[384,128]{1,0:T(8,128)(2,1)S(1)} %collective-permute-done.56.rest_3_) | copy-start | bytes 294916 | tf_op jit(solution)/shard_map/cond
  104.1 14.5 %collective-permute-start.60 = (bf16[2048,128]{1,0:T(8,128)(2,1)S(1)}, bf16[2048,128]{1,0:T(8,128)(2,1)}, u32[]{:S(2)}, u32[]{:S(2)}) collective-permute-start(bf16[2048,128]{1,0:T(8,128)(2,1)S(1)} %get-tuple-element.85.rest_0_), channel_id=1, source_target_pairs={{1,2},{5,6},{9,10},{13,14},{17,18},{21,22},{25,26},{29,30}} | collective-permute-start | bytes 1572872 | tf_op jit(solution)/shard_map/cond/branch_0_fun/ppermute | solution.py:654
  118.6 49.8 %collective-permute-start.69 = (bf16[6144,128]{1,0:T(8,128)(2,1)}, bf16[6144,128]{1,0:T(8,128)(2,1)}, u32[]{:S(2)}, u32[]{:S(2)}) collective-permute-start(bf16[6144,128]{1,0:T(8,128)(2,1)} %collective-permute-done.59.rest_1_), channel_id=1, source_target_pairs={{2,1},{6,5},{10,9},{14,13},{18,17},{22,21},{26,25},{30,29}} | collective-permute-start | bytes 4718600 | tf_op jit(solution)/shard_map/cond/branch_0_fun/ppermute | solution.py:654
  121.1 13.5 %collective-permute-start.61 = (bf16[2048,128]{1,0:T(8,128)(2,1)S(1)}, bf16[2048,128]{1,0:T(8,128)(2,1)}, u32[]{:S(2)}, u32[]{:S(2)}) collective-permute-start(bf16[2048,128]{1,0:T(8,128)(2,1)S(1)} %get-tuple-element.89.rest_0_), channel_id=1, source_target_pairs={{1,2},{5,6},{9,10},{13,14},{17,18},{21,22},{25,26},{29,30}} | collective-permute-start | bytes 1572872 | tf_op jit(solution)/shard_map/cond/branch_0_fun/ppermute | solution.py:654
  122.4 20.8 %collective-permute-start.63 = (bf16[2048,128]{1,0:T(8,128)(2,1)}, bf16[2048,128]{1,0:T(8,128)(2,1)}, u32[]{:S(2)}, u32[]{:S(2)}) collective-permute-start(bf16[2048,128]{1,0:T(8,128)(2,1)} %collective-permute-done.60.rest_1_), channel_id=1, source_target_pairs={{2,3},{6,7},{10,11},{14,15},{18,19},{22,23},{26,27},{30,31}} | collective-permute-start | bytes 1572872 | tf_op jit(solution)/shard_map/cond/branch_0_fun/ppermute | solution.py:654
  134.6 12.5 %collective-permute-start.62 = (bf16[1024,128]{1,0:T(8,128)(2,1)S(1)}, bf16[1024,128]{1,0:T(8,128)(2,1)}, u32[]{:S(2)}, u32[]{:S(2)}) collective-permute-start(bf16[1024,128]{1,0:T(8,128)(2,1)S(1)} %slice.22.rest_0_), channel_id=1, source_target_pairs={{1,2},{5,6},{9,10},{13,14},{17,18},{21,22},{25,26},{29,30}} | collective-permute-start | bytes 786440 | tf_op jit(solution)/shard_map/cond/branch_0_fun/ppermute | solution.py:654
  135.9 11.2 %collective-permute-start.54 = (bf16[1024,128]{1,0:T(8,128)(2,1)S(1)}, bf16[1024,128]{1,0:T(8,128)(2,1)}, u32[]{:S(2)}, u32[]{:S(2)}) collective-permute-start(bf16[1024,128]{1,0:T(8,128)(2,1)S(1)} %slice.20), channel_id=1, source_target_pairs={{0,1},{4,5},{8,9},{12,13},{16,17},{20,21},{24,25},{28,29}} | collective-permute-start | bytes 786440 | tf_op jit(solution)/shard_map/cond/branch_0_fun/ppermute | solution.py:654
  137.2 12.5 %collective-permute-start.65 = (bf16[2048,128]{1,0:T(8,128)(2,1)}, bf16[2048,128]{1,0:T(8,128)(2,1)}, u32[]{:S(2)}, u32[]{:S(2)}) collective-permute-start(bf16[2048,128]{1,0:T(8,128)(2,1)} %collective-permute-done.61.rest_1_), channel_id=1, source_target_pairs={{2,3},{6,7},{10,11},{14,15},{18,19},{22,23},{26,27},{30,31}} | collective-permute-start | bytes 1572872 | tf_op jit(solution)/shard_map/cond/branch_0_fun/ppermute | solution.py:654
  143.2 6.5 %copy-start = (bf16[512,256]{1,0:T(8,128)(2,1)}, bf16[512,256]{1,0:T(8,128)(2,1)S(1)}, u32[]{:S(2)}) copy-start(bf16[512,256]{1,0:T(8,128)(2,1)S(1)} %get-tuple-element.99.weights_ref.token_ref) | copy-start | bytes 786436 | tf_op jit(solution)/shard_map/cond
  143.2 6.5 %copy-start.31 = (bf16[12288,128]{1,0:T(8,128)(2,1)S(1)}, bf16[12288,128]{1,0:T(8,128)(2,1)}, u32[]{:S(2)}) copy-start(bf16[12288,128]{1,0:T(8,128)(2,1)} %get-tuple-element.30.slab_ref) | copy-start | bytes 9437188 | tf_op jit(solution)/shard_map/cond
  147.1 8.5 %collective-permute-start.64 = (bf16[1024,128]{1,0:T(8,128)(2,1)}, bf16[1024,128]{1,0:T(8,128)(2,1)S(1)}, u32[]{:S(2)}, u32[]{:S(2)}) collective-permute-start(bf16[1024,128]{1,0:T(8,128)(2,1)} %collective-permute-done.54.rest_3_), channel_id=1, source_target_pairs={{1,2},{5,6},{9,10},{13,14},{17,18},{21,22},{25,26},{29,30}} | collective-permute-start | bytes 786440 | tf_op jit(solution)/shard_map/cond/branch_0_fun/ppermute | solution.py:654
  148.4 30.3 %collective-permute-start.70 = (bf16[1024,128]{1,0:T(8,128)(2,1)}, bf16[1024,128]{1,0:T(8,128)(2,1)S(1)}, u32[]{:S(2)}, u32[]{:S(2)}) collective-permute-start(bf16[1024,128]{1,0:T(8,128)(2,1)} %collective-permute-done.62.rest_1_), channel_id=1, source_target_pairs={{2,3},{6,7},{10,11},{14,15},{18,19},{22,23},{26,27},{30,31}} | collective-permute-start | bytes 786440 | tf_op jit(solution)/shard_map/cond/branch_0_fun/ppermute | solution.py:654
  149.7 7.4 %copy-start.54 = (f32[2,96,96]{2,1,0:T(8,128)S(1)}, f32[2,96,96]{2,1,0:T(8,128)}, u32[]{:S(2)}) copy-start(f32[2,96,96]{2,1,0:T(8,128)} %get-tuple-element.110.rest_0_) | copy-start | bytes 221188 | tf_op jit(solution)/shard_map/cond
  153.6 2.0 %copy-start.35 = (bf16[12288,128]{1,0:T(8,128)(2,1)}, bf16[12288,128]{1,0:T(8,128)(2,1)S(1)}, u32[]{:S(2)}) copy-start(bf16[12288,128]{1,0:T(8,128)(2,1)S(1)} %get-tuple-element.113.rest_3_) | copy-start | bytes 9437188 | tf_op jit(solution)/shard_map/cond
  155.6 23.1 %collective-permute-start.71 = (bf16[1024,128]{1,0:T(8,128)(2,1)S(1)}, bf16[1024,128]{1,0:T(8,128)(2,1)S(1)}, u32[]{:S(2)}, u32[]{:S(2)}) collective-permute-start(bf16[1024,128]{1,0:T(8,128)(2,1)S(1)} %collective-permute-done.64.rest_4_), channel_id=1, source_target_pairs={{2,3},{6,7},{10,11},{14,15},{18,19},{22,23},{26,27},{30,31}} | collective-permute-start | bytes 786440 | tf_op jit(solution)/shard_map/cond/branch_0_fun/ppermute | solution.py:654
  157.2 2.0 %collective-permute-start.66 = (f32[2,96,96]{2,1,0:T(8,128)S(1)}, f32[2,96,96]{2,1,0:T(8,128)S(1)}, u32[]{:S(2)}, u32[]{:S(2)}) collective-permute-start(f32[2,96,96]{2,1,0:T(8,128)S(1)} %copy-done.54), channel_id=1, source_target_pairs={{0,1},{4,5},{8,9},{12,13},{16,17},{20,21},{24,25},{28,29}} | collective-permute-start | bytes 221192 | tf_op jit(solution)/shard_map/cond/branch_0_fun/ppermute | solution.py:759
  157.9 7.4 %collective-permute-start.67 = (f32[2,96,96]{2,1,0:T(8,128)S(1)}, f32[2,96,96]{2,1,0:T(8,128)S(1)}, u32[]{:S(2)}, u32[]{:S(2)}) collective-permute-start(f32[2,96,96]{2,1,0:T(8,128)S(1)} %copy-done.54), channel_id=1, source_target_pairs={{0,2},{4,6},{8,10},{12,14},{16,18},{20,22},{24,26},{28,30}} | collective-permute-start | bytes 221192 | tf_op jit(solution)/shard_map/cond/branch_0_fun/ppermute | solution.py:759
  159.2 6.1 %copy-start.59 = (f32[2,96,96]{2,1,0:T(8,128)}, f32[2,96,96]{2,1,0:T(8,128)S(1)}, u32[]{:S(2)}) copy-start(f32[2,96,96]{2,1,0:T(8,128)S(1)} %collective-permute-done.66.rest_1_) | copy-start | bytes 221188 | tf_op jit(solution)/shard_map/cond
  159.2 6.1 %collective-permute-start.68 = (f32[2,96,96]{2,1,0:T(8,128)S(1)}, f32[2,96,96]{2,1,0:T(8,128)S(1)}, u32[]{:S(2)}, u32[]{:S(2)}) collective-permute-start(f32[2,96,96]{2,1,0:T(8,128)S(1)} %copy-done.54), channel_id=1, source_target_pairs={{0,3},{4,7},{8,11},{12,15},{16,19},{20,23},{24,27},{28,31}} | collective-permute-start | bytes 221192 | tf_op jit(solution)/shard_map/cond/branch_0_fun/ppermute | solution.py:759
  170.1 8.5 %copy-start.2 = (bf16[512,256]{1,0:T(8,128)(2,1)S(1)}, bf16[512,256]{1,0:T(8,128)(2,1)}, u32[]{:S(2)}) copy-start(bf16[512,256]{1,0:T(8,128)(2,1)} %copy-done) | copy-start | bytes 786436 | tf_op jit(solution)/shard_map/cond
  170.1 8.6 %copy-start.32 = (bf16[12288,128]{1,0:T(8,128)(2,1)S(1)}, bf16[12288,128]{1,0:T(8,128)(2,1)}, u32[]{:S(2)}) copy-start(bf16[12288,128]{1,0:T(8,128)(2,1)} %get-tuple-element.30.slab_ref) | copy-start | bytes 9437188 | tf_op jit(solution)/shard_map/cond
  (10 other events, 8.3 us)
